TPU v7x, 256 devices: a whole 4x4x8 slice. The times are simulated.
256 devices in a mesh: cuts: 8 (over x, y_hi), fsdp: 32 (over z, y_lo, core).
Axes of the slice: x: 4, y: 4 (y_hi: 2, y_lo: 2; y = y_hi * 2 + y_lo), z: 8, core: 2. Of those that a mesh axis runs over, the one named last changes fastest.
Arguments:
- local_params: bfloat16 [8, 32, 128, 8192], P('cuts', 'fsdp'), may hold values from -6 to 6
- outer_params: bfloat16 [32, 128, 8192], P('fsdp'), may hold values from -6 to 6
- column_signs: int32 [8192], replicated, may hold values from 0 to 1
- delta_exponents: int32 [8, 32, 128, 64], P('cuts', 'fsdp'), may hold values from -8 to -6
- outer_master: float32 [32, 128, 8192], P(None, 'cuts', 'fsdp'), may hold values from -6 to 6
- outer_momentum: float32 [32, 128, 8192], P(None, 'cuts', 'fsdp'), may hold values from -3 to 3
- master_exponents: int32 [32, 128, 64], P(None, 'cuts', 'fsdp'), may hold values from -8 to -6
Outputs:
- outer_new: bfloat16 [32, 128, 8192], P('fsdp')
- master_new: float32 [32, 128, 8192], P(None, 'cuts', 'fsdp')
- momentum_new: float32 [32, 128, 8192], P(None, 'cuts', 'fsdp')
All inputs are finite; a program needn't handle non-finite values.
Results may differ from a plain program's by a relative error of at most 0.013.
Values may be sent and summed in bfloat16 or wider, within the bound.
A program may use at most 64 MiB of HBM per device.

v0:
```python
import math

import jax
import jax.numpy as jnp
from jax import lax
from jax.sharding import PartitionSpec as P

HB = 128


CLIP_LIMIT = 448.0
OUTER_RATE = 0.7
MOMENTUM_DECAY = 0.9


def hadamard_table(order):
    index = jnp.arange(order, dtype=jnp.int32)
    parity = jnp.zeros((order, order), jnp.int32)
    for bit_number in range(order.bit_length() - 1):
        row_bits = jnp.bitwise_and(jnp.right_shift(index, bit_number), 1)
        parity = parity + row_bits[:, None] * row_bits[None, :]
    signed = 1 - 2 * jnp.bitwise_and(parity, 1)
    return signed.astype(jnp.float32) * (1.0 / math.sqrt(order))


def rotate_blocks(values, table):
    shaped = values.reshape(values.shape[:-1] + (values.shape[-1] // HB, HB))
    turned = jnp.einsum("...k,kj->...j", shaped, table, precision=lax.Precision.HIGHEST)
    return turned.reshape(values.shape)


def block_scale(values, exponents):
    shaped = values.reshape(values.shape[:-1] + (exponents.shape[-1], HB))
    factor = jnp.exp2(exponents.astype(jnp.float32))
    return (shaped * factor[..., None]).reshape(values.shape)


def encode(values, flips, exponents, table):
    rotated = rotate_blocks(values * flips, table)
    scaled = block_scale(rotated, -exponents)
    return jnp.clip(scaled, -CLIP_LIMIT, CLIP_LIMIT).astype(jnp.bfloat16)


def decode_rotated(encoded, exponents):
    return block_scale(encoded.astype(jnp.float32), exponents)


def unrotate(values, flips, table):
    return rotate_blocks(values, table) * flips


def shards(
    local_params,
    outer_params,
    column_signs,
    delta_exponents,
    outer_master,
    outer_momentum,
    master_exponents,
):
    table = hadamard_table(HB)
    flips = (1 - 2 * column_signs).astype(jnp.float32)
    delta = outer_params.astype(jnp.float32)[None] - local_params.astype(jnp.float32)
    encoded = encode(delta, flips, delta_exponents, table)
    replicas = lax.axis_size("cuts")
    arrived, arrived_exps = (
        lax.all_to_all(
            lax.all_to_all(encoded, "fsdp", split_axis=3, concat_axis=1, tiled=True),
            "cuts",
            split_axis=2,
            concat_axis=0,
            tiled=True,
        ),
        lax.all_to_all(
            lax.all_to_all(delta_exponents, "fsdp", split_axis=3, concat_axis=1, tiled=True),
            "cuts",
            split_axis=2,
            concat_axis=0,
            tiled=True,
        ),
    )
    summed = jnp.sum(decode_rotated(arrived, arrived_exps), axis=0)
    block_width = summed.shape[-1]
    column_start = lax.axis_index("fsdp") * block_width
    own_flips = lax.dynamic_slice_in_dim(flips, column_start, block_width, 0)
    gradient = unrotate(summed / replicas, own_flips, table)
    momentum_new = MOMENTUM_DECAY * outer_momentum + gradient
    master_new = outer_master - OUTER_RATE * (gradient + MOMENTUM_DECAY * momentum_new)
    encoded_new = encode(master_new, own_flips, master_exponents, table)
    gathered, gathered_exps = (
        lax.all_gather(encoded_new, "cuts", axis=1, tiled=True),
        lax.all_gather(master_exponents, "cuts", axis=1, tiled=True),
    )
    landed, landed_exps = (
        lax.all_to_all(gathered, "fsdp", split_axis=0, concat_axis=2, tiled=True),
        lax.all_to_all(gathered_exps, "fsdp", split_axis=0, concat_axis=2, tiled=True),
    )
    outer_new = unrotate(decode_rotated(landed, landed_exps), flips, table).astype(jnp.bfloat16)
    return (outer_new, master_new, momentum_new)


def solution(mesh):
    placed = (
        P("cuts", "fsdp", None, None),
        P("fsdp", None, None),
        P(),
        P("cuts", "fsdp", None, None),
        P(None, "cuts", "fsdp"),
        P(None, "cuts", "fsdp"),
        P(None, "cuts", "fsdp"),
    )
    return jax.shard_map(
        shards,
        mesh=mesh,
        in_specs=placed,
        out_specs=(P("fsdp", None, None), P(None, "cuts", "fsdp"), P(None, "cuts", "fsdp")),
        check_vma=False,
    )
```

profile of v0, /device:TPU:200, one launch (start us, length us, event | category | flops | bytes accessed | tf_op | source)
XLA Modules:
  0.0 378.5 jit_solution(5636192572589384853)
XLA Ops:
  7.2 7.4 %all-to-all-start.2 = ((s32[1,1,128,64]{2,1,0,3:T(1,128)}), s32[1,1,128,64]{2,1,0,3:T(1,128)S(1)}, u32[]{:S(2)}, u32[]{:S(2)}) async-start(s32[1,1,128,64]{2,1,0,3:T(1,128)} %bitcast.106), calls=%async_computation.2 | async-start | bytes 65536 | tf_op jit(solution)/shard_map/all_to_all | solution.py:75
  14.6 0.8 exponential_bitcast_fusion
  15.4 0.8 subtract_convert_fusion
  16.2 2.8 fusion.3
  19.0 0.7 copy.113
  19.7 7.8 %clamp_convert_fusion = bf16[128,64,128]{0,2,1:T(8,128)(2,1)S(1)} fusion(f32[128,64,128]{2,1,0:T(8,128)S(1)} %bitcast.96, f32[128,64]{0,1:T(8,128)S(1)} %exponential_bitcast_fusion, s32[128]{0:T(128)S(1)} %get-tuple-element.6, s32[128]{0:T(128)S(1)} %get-tuple-element.7, s32[128]{0:T(128)S(1)} %get-tuple-element.8, s32[128]{0:T(128)S(1)} %get-tuple-element.9, ...), kind=kOutput, calls=%fused_computation.12 | convolution fusion | flops 1614053376 | bytes 6327808 | tf_op jit(solution)/shard_map/...k,kj->...j/dot_general | solution.py:28
  27.6 33.3 %copy.136 = bf16[1,1,128,8192]{2,1,0,3:T(2,128)(2,1)} copy(bf16[1,1,128,8192]{2,3,1,0:T(8,128)(2,1)S(1)} %bitcast.97) | data formatting | bytes 4194304 | tf_op jit(solution)/shard_map/convert_element_type | solution.py:41
  60.9 0.5 broadcast.237
  61.4 45.4 %reduce.3 = bf16[8192,128]{1,0:T(8,128)(2,1)S(1)} reduce(bf16[8192,1,1,128]{3,2,1,0:T(2,128)(2,1)} %bitcast.92, bf16[]{:T(256)} %broadcast.237), dimensions={1,2}, to_apply=%bitcast.91.reduce_sub_computation | reduce | bytes 4194306
  106.7 2.0 reshape.251
  108.7 8.3 %all-to-all-start = ((bf16[32,2,16384]{2,1,0:T(2,128)(2,1)}), bf16[32,2,16384]{2,1,0:T(2,128)(2,1)S(1)}, u32[]{:S(2)}, u32[]{:S(2)}) async-start(bf16[32,2,16384]{2,1,0:T(2,128)(2,1)} %reshape.251), calls=%async_computation | async-start | bytes 4194304 | tf_op jit(solution)/shard_map/all_to_all | solution.py:68
  117.0 0.1 copy.87
  117.2 0.8 reshape.249
  117.9 47.5 %all-to-all-done = bf16[32,2,16384]{2,1,0:T(2,128)(2,1)S(1)} async-done(((bf16[32,2,16384]{2,1,0:T(2,128)(2,1)}), bf16[32,2,16384]{2,1,0:T(2,128)(2,1)S(1)}, u32[]{:S(2)}, u32[]{:S(2)}) %all-to-all-start) | async-done | bytes 2097184 | tf_op jit(solution)/shard_map/all_to_all | solution.py:68
  165.4 6.0 %all-to-all-start.3 = ((s32[8,1,1024]{2,1,0:T(1,128)}), s32[8,1,1024]{2,1,0:T(1,128)S(1)}, u32[]{:S(2)}, u32[]{:S(2)}) async-start(s32[8,1,1024]{2,1,0:T(1,128)} %reshape.249), calls=%async_computation.3 | async-start | bytes 65536 | tf_op jit(solution)/shard_map/all_to_all | solution.py:74
  171.5 6.8 %reshape.252 = bf16[8192,1,1,128]{3,2,1,0:T(2,128)(2,1)} reshape(bf16[32,2,16384]{2,1,0:T(2,128)(2,1)S(1)} %all-to-all-done) | data formatting | bytes 4194304
  178.3 2.5 copy.108
  180.7 2.9 copy.84
  183.6 7.2 %all-to-all-start.1 = ((bf16[1,32,128,256]{3,1,0,2:T(8,128)(2,1)}), bf16[1,32,128,256]{3,1,0,2:T(8,128)(2,1)}, u32[]{:S(2)}, u32[]{:S(2)}) async-start(bf16[1,32,128,256]{3,1,0,2:T(8,128)(2,1)} %copy.84), calls=%async_computation.1 | async-start | bytes 4194304 | tf_op jit(solution)/shard_map/all_to_all | solution.py:67
  190.8 0.0 all-gather.2.cloned.1.call-start
  190.9 0.1 dynamic_slice.3
  191.0 0.1 copy.96
  191.1 0.5 broadcast.236
  191.6 0.7 reduce.2
  192.3 0.2 reshape.250
  192.5 0.1 copy.88
  192.6 0.6 copy.105
  193.2 6.6 %mul.375 = f32[8,32,16,2,128]{4,3,2,0,1:T(2,128)} broadcast(f32[8,32,16,2]{3,2,0,1:T(8,128)S(1)} %bitcast.99), dimensions={0,1,2,3} | broadcast | bytes 4227072 | tf_op jit(solution)/shard_map/mul | solution.py:35
  199.8 6.4 %mul.376 = f32[8,1,32,16,256]{4,3,0,2,1:T(8,128)} reshape(f32[8,32,16,2,128]{4,3,2,0,1:T(2,128)} %mul.375) | data formatting | bytes 8388608 | tf_op jit(solution)/shard_map/mul | solution.py:35
  206.2 15.1 %all-to-all-done.1 = bf16[1,32,128,256]{3,1,0,2:T(8,128)(2,1)} async-done(((bf16[1,32,128,256]{3,1,0,2:T(8,128)(2,1)}), bf16[1,32,128,256]{3,1,0,2:T(8,128)(2,1)}, u32[]{:S(2)}, u32[]{:S(2)}) %all-to-all-start.1) | async-done | bytes 2097184 | tf_op jit(solution)/shard_map/all_to_all | solution.py:67
  221.4 2.9 copy.85
  224.3 0.7 fusion.1
  225.1 0.7 convolution_bitcast_fusion
  225.8 1.2 multiply_bitcast_fusion
  227.0 0.7 fusion.13
  227.8 0.7 copy.135
  228.5 0.0 all-gather.2.cloned.1.call-update
  228.5 34.3 %all_gather.7 = s32[32,128,2]{0,2,1:T(2,128)S(1)} all-gather(s32[32,16,2]{0,2,1:T(2,128)S(1)} %copy-done.3), channel_id=1, replica_groups=mesh['cuts'=8,'fsdp'=32] {'cuts'}, dimensions={1}, use_global_device_ids=true | all-gather | bytes 36864 | tf_op jit(solution)/shard_map/all_gather | solution.py:92
  262.8 0.1 copy.99
  262.9 10.7 %all_to_all.72 = s32[32,128,2]{1,2,0:T(2,128)S(1)} all-to-all(s32[32,128,2]{1,2,0:T(2,128)S(1)} %copy.99), channel_id=1, replica_groups=mesh['cuts'=8,'fsdp'=32] {'fsdp'}, dimensions={0} | all-to-all | bytes 65536 | tf_op jit(solution)/shard_map/all_to_all | solution.py:96
  273.6 15.7 %all-gather.2.cloned.1.call-done = bf16[32,128,256]{2,1,0:T(8,128)(2,1)} async-done(((bf16[32,16,256]{2,1,0:T(8,128)(2,1)}), bf16[32,128,256]{2,1,0:T(8,128)(2,1)}) %all-gather.2.cloned.1.call-update) | async-done | bytes 2097168 | tf_op jit(solution)/shard_map/all_gather | solution.py:91
  289.3 8.1 %all-to-all-start.4 = ((bf16[32,128,256]{2,1,0:T(8,128)(2,1)}), bf16[32,128,256]{2,1,0:T(8,128)(2,1)S(1)}, u32[]{:S(2)}, u32[]{:S(2)}) async-start(bf16[32,128,256]{2,1,0:T(8,128)(2,1)} %all-gather.2.cloned.1.call-done), calls=%async_computation.4 | async-start | bytes 4194304 | tf_op jit(solution)/shard_map/all_to_all | solution.py:95
  297.5 48.4 %all-to-all-done.4 = bf16[32,128,256]{2,1,0:T(8,128)(2,1)S(1)} async-done(((bf16[32,128,256]{2,1,0:T(8,128)(2,1)}), bf16[32,128,256]{2,1,0:T(8,128)(2,1)S(1)}, u32[]{:S(2)}, u32[]{:S(2)}) %all-to-all-start.4) | async-done | bytes 2097184 | tf_op jit(solution)/shard_map/all_to_all | solution.py:95
  345.9 2.5 convert_bitcast_fusion
  348.4 5.6 %copy.98 = f32[1,128,32,256]{1,3,2,0:T(8,128)} copy(f32[1,128,32,256]{3,1,2,0:T(8,128)} %convert_bitcast_fusion) | data formatting | bytes 8388608 | tf_op jit(solution)/shard_map/convert_element_type | solution.py:45
  353.9 8.3 %fusion.6 = f32[128,64,128]{0,2,1:T(8,128)} fusion(f32[128,64,128]{0,2,1:T(8,128)} %bitcast.94, f32[128,64]{0,1:T(8,128)S(1)} %bitcast.104, s32[128]{0:T(128)S(1)} %get-tuple-element.6, s32[128]{0:T(128)S(1)} %get-tuple-element.7, s32[128]{0:T(128)S(1)} %get-tuple-element.8, s32[128]{0:T(128)S(1)} %get-tuple-element.9, s32[128]{0:T(128)S(1)} %get-tuple-element.10, ...), kind=kOutput, calls=%fused_computation.10 | convolution fusion | flops 1611956224 | bytes 8424960 | tf_op jit(solution)/shard_map/...k,kj->...j/dot_general | solution.py:28
  362.2 5.6 %copy.101 = f32[1,128,8192]{2,1,0:T(8,128)} copy(f32[1,128,8192]{1,2,0:T(8,128)} %bitcast.95) | data formatting | bytes 8388608 | tf_op jit(solution)/shard_map/reshape | solution.py:29
  367.8 3.8 %multiply_convert_fusion = bf16[1,128,8192]{2,1,0:T(8,128)(2,1)} fusion(f32[1,128,8192]{2,1,0:T(8,128)} %copy.101, f32[8192]{0:T(1024)S(1)} %subtract_convert_fusion), kind=kLoop, calls=%fused_computation.9 | loop fusion | flops 2097152 | bytes 6324224 | tf_op jit(solution)/shard_map/convert_element_type | solution.py:98
  (17 shorter events, 0.1 us)
Async XLA Ops:
  7.2 101.6 %all-to-all-start.2 = ((s32[1,1,128,64]{2,1,0,3:T(1,128)}), s32[1,1,128,64]{2,1,0,3:T(1,128)S(1)}, u32[]{:S(2)}, u32[]{:S(2)}) async-start(s32[1,1,128,64]{2,1,0,3:T(1,128)} %bitcast.106), calls=%async_computation.2 | async-start | bytes 65536 | tf_op jit(solution)/shard_map/all_to_all | solution.py:75
  108.7 56.7 %all-to-all-start = ((bf16[32,2,16384]{2,1,0:T(2,128)(2,1)}), bf16[32,2,16384]{2,1,0:T(2,128)(2,1)S(1)}, u32[]{:S(2)}, u32[]{:S(2)}) async-start(bf16[32,2,16384]{2,1,0:T(2,128)(2,1)} %reshape.251), calls=%async_computation | async-start | bytes 4194304 | tf_op jit(solution)/shard_map/all_to_all | solution.py:68
  165.4 18.2 %all-to-all-start.3 = ((s32[8,1,1024]{2,1,0:T(1,128)}), s32[8,1,1024]{2,1,0:T(1,128)S(1)}, u32[]{:S(2)}, u32[]{:S(2)}) async-start(s32[8,1,1024]{2,1,0:T(1,128)} %reshape.249), calls=%async_computation.3 | async-start | bytes 65536 | tf_op jit(solution)/shard_map/all_to_all | solution.py:74
  180.7 10.2 %copy-start.3 = (s32[32,16,2]{0,2,1:T(2,128)S(1)}, s32[32,16,2]{0,2,1:T(2,128)}, u32[]{:S(2)}) copy-start(s32[32,16,2]{0,2,1:T(2,128)} %param.13) | copy-start | bytes 12292
  183.6 37.7 %all-to-all-start.1 = ((bf16[1,32,128,256]{3,1,0,2:T(8,128)(2,1)}), bf16[1,32,128,256]{3,1,0,2:T(8,128)(2,1)}, u32[]{:S(2)}, u32[]{:S(2)}) async-start(bf16[1,32,128,256]{3,1,0,2:T(8,128)(2,1)} %copy.84), calls=%async_computation.1 | async-start | bytes 4194304 | tf_op jit(solution)/shard_map/all_to_all | solution.py:67
  190.8 98.5 %all-gather.2.cloned.1.call-start = ((), (), s32[]{:S(2)}) async-start(), calls=%async_computation.6 | async-start | bytes 2359296 | tf_op jit(solution)/shard_map/all_gather | solution.py:91
  221.4 2.9 copy-start
  224.3 1.5 copy-start.1
  224.3 1.5 copy-start.2
  289.3 56.5 %all-to-all-start.4 = ((bf16[32,128,256]{2,1,0:T(8,128)(2,1)}), bf16[32,128,256]{2,1,0:T(8,128)(2,1)S(1)}, u32[]{:S(2)}, u32[]{:S(2)}) async-start(bf16[32,128,256]{2,1,0:T(8,128)(2,1)} %all-gather.2.cloned.1.call-done), calls=%async_computation.4 | async-start | bytes 4194304 | tf_op jit(solution)/shard_map/all_to_all | solution.py:95
Sparse Core Ops, SparseCore 0:
  228.7 60.6 all-gather.1
where the time goes:
time: 385 us; the launch traced here: 379 us
  waiting for transfers between devices  127 us (33%)
  local copies, waits for them, and re-layouts  79.1 us (21%)
  other arithmetic  58.8 us (15%)
  blocking collectives  45 us (12%)
  starting transfers between devices  37.1 us (10%)
  matrix products  17.6 us (5%)
  between operations  14.2 us (4%)
    unnamed x3, other arithmetic  49.4 us
    all_to_all x1, waiting for transfers between devices, shards(): lax.all_to_all(gathered, 'fsdp', split_axis=0, concat_axis=2, tiled=True)  48.4 us
    all_to_all x1, waiting for transfers between devices, shards(): lax.all_to_all(encoded, 'fsdp', split_axis=3, concat_axis=1, tiled=True)  47.5 us
    all_gather x1, blocking collectives, shards(): lax.all_gather(master_exponents, 'cuts', axis=1, tiled=True)  34.3 us
    convert_element_type x2, local copies, waits for them, and re-layouts, encode(): return jnp.clip(scaled, -CLIP_LIMIT, CLIP_LIMIT).astype(jnp.bfloat16)  34 us
    dot_general x4, matrix products, rotate_blocks(): jnp.einsum('...k,kj->...j', shaped, table, precision=lax.Precision.HIGHEST)  17.6 us
    all_gather x1, waiting for transfers between devices, shards(): lax.all_gather(encoded_new, 'cuts', axis=1, tiled=True)  15.7 us
    all_to_all x1, waiting for transfers between devices, shards(): lax.all_to_all(lax.all_to_all(encoded, 'fsdp', split_axis=3, concat_axis=...  15.1 us
  transfers between devices with their start and end apart: 6, of which 4 were waited for; matrix products, arithmetic and copies ran while one was open for 32% of the time, Pallas kernels for 0%

commit v1 on v0

v1 whole, which is shorter than its diff:
```python
import functools
import math

import jax
import jax.numpy as jnp
from jax import lax
from jax.experimental import pallas as pl
from jax.experimental.pallas import tpu as pltpu
from jax.sharding import PartitionSpec as P

HB = 128
RB = 16
OW = 256
CUTS = 8
FSDP = 32
DIM = FSDP * OW
ROWS = CUTS * RB
LIMIT = 448.0 * math.sqrt(HB)
OUTER_RATE = 0.7
DECAY = 0.9
KEEP_MOMENTUM = OUTER_RATE * DECAY * DECAY
GRAD_IN_MASTER = OUTER_RATE * (1.0 + DECAY)
MESH = pl.DeviceIdType.MESH

XA, XB, YH = 0, 1, 2
ORDERS = ((XA, XB, YH), (XB, YH, XA), (YH, XA, XB))
SIZES = (6, 5, 5, 5, 6, 5)


def column_groups():
    groups, start = [], 0
    for k, n in enumerate(SIZES):
        groups.append((start, n, ORDERS[k % 3]))
        start += n
    assert start == FSDP
    return groups


GROUPS = column_groups()
NG = len(GROUPS)


def sylvester(order):
    i = lax.broadcasted_iota(jnp.int32, (order, order), 0)
    j = lax.broadcasted_iota(jnp.int32, (order, order), 1)
    t = jnp.bitwise_and(i, j)
    for s in (4, 2, 1):
        t = jnp.bitwise_xor(t, jnp.right_shift(t, s))
    return (1 - 2 * jnp.bitwise_and(t, 1)).astype(jnp.float32)


def power(exponents):
    return jnp.exp2(exponents.astype(jnp.float32)).astype(jnp.bfloat16)


def kernel(
    local_hbm, outer_hbm, signs_hbm, dexp_hbm, master_hbm, mom_hbm, mexp_hbm,
    out_hbm, master_out, mom_out,
    lv, ov, sv, so, dexp_v, thr, master_v, mom_v, mexp_v, master_o, mom_o,
    w1, bd, asrc, abuf, sbuf, srecv,
    *rest,
):
    parts, r1, r2, r3, res = (rest[k * NG:(k + 1) * NG] for k in range(5))
    (ld_sem, in_sem, rs_send, rs_recv, ag_send, ag_recv, a1_sem, a2_sem, out_sem) = rest[5 * NG:]
    c, f = lax.axis_index("cuts"), lax.axis_index("fsdp")
    x, yh = lax.div(c, 2), lax.rem(c, 2)
    v = lax.div(x, 2)
    u = lax.rem(lax.rem(x, 2) + v, 2)
    flip_x = x + 1 - 2 * lax.rem(x, 2)
    partner = (
        (flip_x * 2 + yh, f),
        ((3 - x) * 2 + yh, f),
        (x * 2 + 1 - yh, f),
    )

    def first_row(order, bits):
        mine = [u, v, yh]
        for d, b in zip(order, bits):
            mine[d] = lax.rem(mine[d] + b, 2)
        au, av, ay = mine
        ax = av * 2 + lax.rem(au + av, 2)
        return pl.multiple_of((ax * 2 + ay) * RB, RB)

    barrier = pltpu.get_barrier_semaphore()
    for p in partner:
        pl.semaphore_signal(barrier, inc=1, device_id=p, device_id_type=MESH)

    @pl.loop(1, FSDP)
    def _(k):
        pl.semaphore_signal(barrier, inc=1, device_id=(c, lax.rem(f + k, FSDP)), device_id_type=MESH)

    small = [
        pltpu.make_async_copy(dexp_hbm.at[0, 0], dexp_v, in_sem.at[0]),
        pltpu.make_async_copy(signs_hbm, sv, in_sem.at[1]),
        pltpu.make_async_copy(signs_hbm.at[:, pl.ds(pl.multiple_of(f * OW, OW), OW)], so, in_sem.at[2]),
        pltpu.make_async_copy(master_hbm, master_v, in_sem.at[3]),
        pltpu.make_async_copy(mom_hbm, mom_v, in_sem.at[4]),
        pltpu.make_async_copy(mexp_hbm, mexp_v, in_sem.at[5]),
    ]
    loads = []
    for g, (start, n, _) in enumerate(GROUPS):
        cols = pl.ds(start * OW, n * OW)
        loads.append((
            pltpu.make_async_copy(local_hbm.at[0, 0, :, cols], lv.at[:, cols], ld_sem.at[g, 0]),
            pltpu.make_async_copy(outer_hbm.at[0, :, cols], ov.at[:, cols], ld_sem.at[g, 1]),
        ))
    small[0].start()
    small[1].start()
    for pair in loads:
        for cp in pair:
            cp.start()
    for cp in small[2:]:
        cp.start()

    table = sylvester(HB)
    table_b = table.astype(jnp.bfloat16)
    w1[0:HB, :] = table_b
    w1[HB:OW, :] = (-table).astype(jnp.bfloat16)
    zero = jnp.zeros((HB, HB), jnp.bfloat16)
    bd[0:HB, 0:HB] = table_b
    bd[HB:OW, HB:OW] = table_b
    bd[0:HB, HB:OW] = zero
    bd[HB:OW, 0:HB] = zero

    small[0].wait()
    thr[...] = power(dexp_v[...]).astype(jnp.float32) * LIMIT
    small[1].wait()

    def deltas(g, half):
        start, n, order = GROUPS[g]

        def block(j, carry):
            row = first_row(order, (half, lax.div(j, 2), lax.rem(j, 2)))
            tiles = []
            for k in range(2 * n):
                cols = pl.ds((2 * start + k) * HB, HB)
                flips = (1 - 2 * sv[:, cols]).astype(jnp.float32).astype(jnp.bfloat16)
                o = ov[pl.ds(row, RB), cols] * flips
                l = lv[pl.ds(row, RB), cols] * flips
                tiles.append(jnp.concatenate([o, l], axis=1))
            turned = jnp.dot(jnp.concatenate(tiles, axis=0), w1[...], preferred_element_type=jnp.float32)
            limits = thr[pl.ds(row, RB), :]
            for k in range(2 * n):
                cb = 2 * start + k
                top = jnp.broadcast_to(limits[:, cb:cb + 1], (RB, HB))
                value = turned[k * RB:(k + 1) * RB, :]
                value = jnp.minimum(jnp.maximum(value, -top), top)
                parts[g][half, j, :, pl.ds(k * HB, HB)] = value.astype(jnp.bfloat16)
            return carry

        lax.fori_loop(0, 4, block, 0)

    def remote(src, dst, send, recv, to):
        return pltpu.make_async_remote_copy(
            src_ref=src, dst_ref=dst, send_sem=send, recv_sem=recv, device_id=to, device_id_type=MESH
        )

    def rs_copy(g, step):
        to = partner[GROUPS[g][2][step]]
        src = (parts[g].at[1], parts[g].at[0, pl.ds(2, 2)], parts[g].at[0, 1])[step]
        dst = (r1[g], r2[g], r3[g])[step]
        return remote(src, dst, rs_send.at[g, step], rs_recv.at[g, step], to)

    def ag_copy(g, step):
        to = partner[GROUPS[g][2][2 - step]]
        src = (res[g].at[0, 0], res[g].at[0, pl.ds(0, 2)], res[g].at[0])[step]
        dst = (res[g].at[0, 1], res[g].at[0, pl.ds(2, 2)], res[g].at[1])[step]
        return remote(src, dst, ag_send.at[g, step], ag_recv.at[g, step], to)

    def add(mine, other):
        return mine.astype(jnp.float32) + other.astype(jnp.float32)

    for g in range(NG):
        for cp in loads[g]:
            cp.wait()
        deltas(g, 1)
        if g == 0:
            pl.semaphore_wait(barrier, 3 + FSDP - 1)
        rs_copy(g, 0).start()

    for cp in small[2:]:
        cp.wait()
    own = (1 - 2 * so[...]).astype(jnp.float32)

    def prepare(k, carry):
        s = pl.ds(k * 8, 8)
        a = (master_v[s] - KEEP_MOMENTUM * mom_v[s]).reshape(8 * RB, OW) * own
        hi = a.astype(jnp.bfloat16)
        lo = (a - hi.astype(jnp.float32)).astype(jnp.bfloat16)
        turned = jnp.dot(hi, bd[...], preferred_element_type=jnp.float32)
        turned += jnp.dot(lo, bd[...], preferred_element_type=jnp.float32)
        asrc[s, :, 0:OW] = turned.astype(jnp.bfloat16).reshape(8, RB, OW)
        e = mexp_v[s]
        first = lax.broadcasted_iota(jnp.int32, (8, RB, HB), 2) < HB // 2
        both = jnp.where(first, e[:, :, 0:1], e[:, :, 1:2])
        asrc[s, :, OW:OW + HB] = power(both)
        return carry

    lax.fori_loop(0, FSDP // 8, prepare, 0)

    @pl.loop(1, FSDP)
    def _(k):
        to = lax.rem(f + k, FSDP)
        remote(asrc.at[to], abuf.at[f], a1_sem.at[0], a1_sem.at[1], (c, to)).start()

    abuf[f] = asrc[f]

    for g in range(NG):
        deltas(g, 0)

    for g in range(NG):
        rs_copy(g, 0).wait_recv()

        def acc1(j, carry):
            parts[g][0, j] = add(parts[g][0, j], r1[g][j]).astype(jnp.bfloat16)
            return carry

        lax.fori_loop(2, 4, acc1, 0)
        rs_copy(g, 1).start()
        lax.fori_loop(0, 2, acc1, 0)
    for g in range(NG):
        rs_copy(g, 1).wait_recv()
        parts[g][0, 1] = add(parts[g][0, 1], r2[g][1]).astype(jnp.bfloat16)
        rs_copy(g, 2).start()
        parts[g][0, 0] = add(parts[g][0, 0], r2[g][0]).astype(jnp.bfloat16)

    whole = pl.ds(0, FSDP - 1)
    pltpu.make_async_copy(abuf.at[whole], abuf.at[whole], a1_sem.at[1]).wait()

    for g, (start, n, order) in enumerate(GROUPS):
        rs_copy(g, 2).wait_recv()
        codes = []
        for k in range(n):
            cols = pl.ds(k * OW, OW)
            total = add(parts[g][0, 0, :, cols], r3[g][:, cols])
            sbuf[start + k] = total.astype(jnp.bfloat16)
            code = abuf[start + k, :, 0:OW].astype(jnp.float32) - (GRAD_IN_MASTER / CUTS) * total
            scale = abuf[start + k, :, OW:OW + HB].astype(jnp.float32) * LIMIT
            top = jnp.concatenate(
                [jnp.broadcast_to(scale[:, 0:1], (RB, HB)), jnp.broadcast_to(scale[:, HB // 2:HB // 2 + 1], (RB, HB))],
                axis=1,
            )
            codes.append(jnp.minimum(jnp.maximum(code, -top), top).astype(jnp.bfloat16))
        turned = jnp.dot(jnp.concatenate(codes, axis=0), bd[...], preferred_element_type=jnp.float32)
        for k in range(n):
            flips = (1 - 2 * sv[:, pl.ds((start + k) * OW, OW)]).astype(jnp.float32) * (1.0 / HB)
            value = turned[k * RB:(k + 1) * RB, :] * flips
            res[g][0, 0, :, pl.ds(k * OW, OW)] = value.astype(jnp.bfloat16)
        ag_copy(g, 0).start()

        @pl.loop(start, start + n)
        def _(to):
            @pl.when(to != f)
            def _():
                remote(sbuf.at[to], srecv.at[f], a2_sem.at[0], a2_sem.at[1], (c, to)).start()

    srecv[f] = sbuf[f]

    def write(g, half, j):
        start, n, order = GROUPS[g]
        row = first_row(order, (half, j // 2, j % 2))
        return pltpu.make_async_copy(
            res[g].at[half, j],
            out_hbm.at[0, pl.ds(row, RB), pl.ds(start * OW, n * OW)],
            out_sem.at[g, half * 4 + j],
        )

    for g in range(NG):
        ag_copy(g, 0).wait_recv()
        ag_copy(g, 1).start()
        write(g, 0, 0).start()
        write(g, 0, 1).start()
    for g in range(NG):
        ag_copy(g, 1).wait_recv()
        ag_copy(g, 2).start()
        write(g, 0, 2).start()
        write(g, 0, 3).start()

    pltpu.make_async_copy(srecv.at[whole], srecv.at[whole], a2_sem.at[1]).wait()

    def finish(k, carry):
        s = pl.ds(k * 8, 8)
        turned = jnp.dot(srecv[s].reshape(8 * RB, OW), bd[...], preferred_element_type=jnp.float32)
        grad = (turned * (own * (1.0 / (HB * CUTS)))).reshape(8, RB, OW)
        mom = DECAY * mom_v[s] + grad
        mom_o[s] = mom
        master_o[s] = master_v[s] - OUTER_RATE * (grad + DECAY * mom)
        return carry

    lax.fori_loop(0, FSDP // 8, finish, 0)
    outs = [
        pltpu.make_async_copy(master_o, master_out, in_sem.at[0]),
        pltpu.make_async_copy(mom_o, mom_out, in_sem.at[1]),
    ]
    for cp in outs:
        cp.start()

    for g in range(NG):
        ag_copy(g, 2).wait_recv()
        for j in range(4):
            write(g, 1, j).start()
    for g in range(NG):
        for step in range(3):
            rs_copy(g, step).wait_send()
            ag_copy(g, step).wait_send()
        for half in range(2):
            for j in range(4):
                write(g, half, j).wait()
    pltpu.make_async_copy(asrc.at[whole], asrc.at[whole], a1_sem.at[0]).wait()
    pltpu.make_async_copy(sbuf.at[whole], sbuf.at[whole], a2_sem.at[0]).wait()
    for cp in outs:
        cp.wait()


def step(local_params, outer_params, column_signs, delta_exponents, outer_master, outer_momentum, master_exponents):
    bf16, f32, i32 = jnp.bfloat16, jnp.float32, jnp.int32
    widths = [n * OW for _, n, _ in GROUPS]
    anywhere = pl.BlockSpec(memory_space=pl.ANY)
    state = (FSDP, RB, OW)
    scratch = [
        pltpu.VMEM((ROWS, DIM), bf16),
        pltpu.VMEM((ROWS, DIM), bf16),
        pltpu.VMEM((1, DIM), i32),
        pltpu.VMEM((1, OW), i32),
        pltpu.VMEM((ROWS, DIM // HB), i32),
        pltpu.VMEM((ROWS, DIM // HB), f32),
        pltpu.VMEM(state, f32),
        pltpu.VMEM(state, f32),
        pltpu.VMEM((FSDP, RB, OW // HB), i32),
        pltpu.VMEM(state, f32),
        pltpu.VMEM(state, f32),
        pltpu.VMEM((OW, HB), bf16),
        pltpu.VMEM((OW, OW), bf16),
        pltpu.VMEM((FSDP, RB, OW + HB), bf16),
        pltpu.VMEM((FSDP, RB, OW + HB), bf16),
        pltpu.VMEM(state, bf16),
        pltpu.VMEM(state, bf16),
    ]
    scratch += [pltpu.VMEM((2, 4, RB, w), bf16) for w in widths]
    scratch += [pltpu.VMEM((4, RB, w), bf16) for w in widths]
    scratch += [pltpu.VMEM((2, RB, w), bf16) for w in widths]
    scratch += [pltpu.VMEM((RB, w), bf16) for w in widths]
    scratch += [pltpu.VMEM((2, 4, RB, w), bf16) for w in widths]
    dma = pltpu.SemaphoreType.DMA
    scratch += [
        dma((NG, 2)), dma((6,)), dma((NG, 3)), dma((NG, 3)), dma((NG, 3)), dma((NG, 3)),
        dma((2,)), dma((2,)), dma((NG, 8)),
    ]
    return pl.pallas_call(
        kernel,
        out_shape=(
            jax.ShapeDtypeStruct((1, ROWS, DIM), bf16),
            jax.ShapeDtypeStruct(state, f32),
            jax.ShapeDtypeStruct(state, f32),
        ),
        in_specs=[anywhere] * 7,
        out_specs=(anywhere,) * 3,
        scratch_shapes=scratch,
        compiler_params=pltpu.CompilerParams(
            collective_id=0, has_side_effects=True, vmem_limit_bytes=40 * 1024 * 1024
        ),
    )(
        local_params, outer_params, column_signs.reshape(1, DIM), delta_exponents,
        outer_master, outer_momentum, master_exponents,
    )


def solution(mesh):
    placed = (
        P("cuts", "fsdp", None, None),
        P("fsdp", None, None),
        P(),
        P("cuts", "fsdp", None, None),
        P(None, "cuts", "fsdp"),
        P(None, "cuts", "fsdp"),
        P(None, "cuts", "fsdp"),
    )
    return jax.shard_map(
        step,
        mesh=mesh,
        in_specs=placed,
        out_specs=(P("fsdp", None, None), P(None, "cuts", "fsdp"), P(None, "cuts", "fsdp")),
        check_vma=False,
    )
```

time: 385 us -> 62.1 us (0.16)
  the two profiles are of different devices: /device:TPU:200 before, /device:TPU:16 now
where the time goes in v1:
time: 62.1 us; the launch traced here: 61.7 us
  Pallas kernels  50.3 us (81%)
  local copies, waits for them, and re-layouts  10.7 us (17%)
  between operations  0.66 us (1%)
    pallas_call x1, Pallas kernels, step(): pl.pallas_call(kernel, out_shape=(jax.ShapeDtypeStruct((1, ROWS, DIM), bf...  50.3 us
    unnamed x15, local copies, waits for them, and re-layouts  10.7 us

profile of v1, /device:TPU:16, one launch (start us, length us, event | category | flops | bytes accessed | tf_op | source)
XLA Modules:
  0.0 61.7 jit_solution(7466646824975343832)
XLA Ops:
  0.6 0.8 %copy.10.dexp_hbm = s32[1,1,128,64]{3,2,1,0:T(8,128)S(1)} copy(s32[1,1,128,64]{2,3,1,0:T(8,128)} %param.10) | data formatting | bytes 65536 | tf_op args[3]
  1.5 0.9 %copy.11.mexp_hbm = s32[32,16,2]{2,1,0:T(8,128)S(1)} copy(s32[32,16,2]{0,2,1:T(2,128)} %param.13) | data formatting | bytes 8192 | tf_op args[6]
  2.4 0.0 copy-start
  2.4 1.6 %copy-done = bf16[1,1,128,8192]{3,2,1,0:T(8,128)(2,1)S(1)} copy-done((bf16[1,1,128,8192]{3,2,1,0:T(8,128)(2,1)S(1)}, bf16[1,1,128,8192]{3,2,1,0:T(8,128)(2,1)}, u32[]{:S(2)}) %copy-start) | copy-done | bytes 2097176
  4.0 0.0 copy-start.1
  4.0 1.6 %copy-done.1 = bf16[1,128,8192]{2,1,0:T(8,128)(2,1)S(1)} copy-done((bf16[1,128,8192]{2,1,0:T(8,128)(2,1)S(1)}, bf16[1,128,8192]{2,1,0:T(8,128)(2,1)}, u32[]{:S(2)}) %copy-start.1) | copy-done | bytes 2097176
  5.6 0.0 copy-start.2
  5.6 1.0 %copy-done.2 = f32[32,16,256]{2,1,0:T(8,128)S(1)} copy-done((f32[32,16,256]{2,1,0:T(8,128)S(1)}, f32[32,16,256]{2,1,0:T(8,128)}, u32[]{:S(2)}) %copy-start.2) | copy-done | bytes 524312
  6.6 0.0 copy-start.3
  6.6 1.0 %copy-done.3 = f32[32,16,256]{2,1,0:T(8,128)S(1)} copy-done((f32[32,16,256]{2,1,0:T(8,128)S(1)}, f32[32,16,256]{2,1,0:T(8,128)}, u32[]{:S(2)}) %copy-start.3) | copy-done | bytes 524312
  7.7 0.0 copy-start.4
  7.7 0.8 %copy-done.4 = s32[8192]{0:T(1024)S(1)} copy-done((s32[8192]{0:T(1024)S(1)}, s32[8192]{0:T(1024)}, u32[]{:S(2)}) %copy-start.4) | copy-done | bytes 32792
  8.4 50.3 %shard_map.94 = (bf16[1,128,8192]{2,1,0:T(8,128)(2,1)S(1)}, f32[32,16,256]{2,1,0:T(8,128)S(1)}, f32[32,16,256]{2,1,0:T(8,128)S(1)}) custom-call(bf16[1,1,128,8192]{3,2,1,0:T(8,128)(2,1)S(1)} %copy-done, bf16[1,128,8192]{2,1,0:T(8,128)(2,1)S(1)} %copy-done.1, s32[1,8192]{1,0:T(1,128)S(1)} %bitcast.1, s32[1,1,128,64]{3,2,1,0:T(8,128)S(1)} %copy.10.dexp_hbm, ...), custom_call_target="tpu_custom_call" | custom-call | tf_op jit(solution)/shard_map/pallas_call | solution.py:349
  58.8 1.3 %copy.15 = bf16[1,128,8192]{2,1,0:T(8,128)(2,1)} copy(bf16[1,128,8192]{2,1,0:T(8,128)(2,1)S(1)} %get-tuple-element.6) | data formatting | bytes 4194304
  60.1 0.8 %copy.16 = f32[32,16,256]{2,1,0:T(8,128)} copy(f32[32,16,256]{2,1,0:T(8,128)S(1)} %get-tuple-element.7) | data formatting | bytes 1048576
  60.9 0.8 %copy.17 = f32[32,16,256]{2,1,0:T(8,128)} copy(f32[32,16,256]{2,1,0:T(8,128)S(1)} %get-tuple-element.8) | data formatting | bytes 1048576
Async XLA Ops:
  2.4 1.6 %copy-start = (bf16[1,1,128,8192]{3,2,1,0:T(8,128)(2,1)S(1)}, bf16[1,1,128,8192]{3,2,1,0:T(8,128)(2,1)}, u32[]{:S(2)}) copy-start(bf16[1,1,128,8192]{3,2,1,0:T(8,128)(2,1)} %local_hbm.1) | copy-start | bytes 6291460
  4.0 1.6 %copy-start.1 = (bf16[1,128,8192]{2,1,0:T(8,128)(2,1)S(1)}, bf16[1,128,8192]{2,1,0:T(8,128)(2,1)}, u32[]{:S(2)}) copy-start(bf16[1,128,8192]{2,1,0:T(8,128)(2,1)} %outer_hbm.1) | copy-start | bytes 6291460
  5.6 1.0 %copy-start.2 = (f32[32,16,256]{2,1,0:T(8,128)S(1)}, f32[32,16,256]{2,1,0:T(8,128)}, u32[]{:S(2)}) copy-start(f32[32,16,256]{2,1,0:T(8,128)} %master_hbm.1) | copy-start | bytes 1572868
  6.6 1.0 %copy-start.3 = (f32[32,16,256]{2,1,0:T(8,128)S(1)}, f32[32,16,256]{2,1,0:T(8,128)}, u32[]{:S(2)}) copy-start(f32[32,16,256]{2,1,0:T(8,128)} %mom_hbm.1) | copy-start | bytes 1572868
  7.7 0.8 %copy-start.4 = (s32[8192]{0:T(1024)S(1)}, s32[8192]{0:T(1024)}, u32[]{:S(2)}) copy-start(s32[8192]{0:T(1024)} %param.9) | copy-start | bytes 98308

commit v2 on v1

v2 whole, which is shorter than its diff:
```python
import functools
import math

import jax
import jax.numpy as jnp
from jax import lax
from jax.experimental import pallas as pl
from jax.experimental.pallas import tpu as pltpu
from jax.sharding import PartitionSpec as P

HB = 128
RB = 16
OW = 256
CUTS = 8
FSDP = 32
DIM = FSDP * OW
ROWS = CUTS * RB
LIMIT = 448.0 * math.sqrt(HB)
OUTER_RATE = 0.7
DECAY = 0.9
KEEP_MOMENTUM = OUTER_RATE * DECAY * DECAY
GRAD_IN_MASTER = OUTER_RATE * (1.0 + DECAY)
MESH = pl.DeviceIdType.MESH

XA, XB, YH = 0, 1, 2
ORDERS = ((XA, XB, YH), (XB, YH, XA), (YH, XA, XB))
SIZES = (6, 5, 5, 6, 5, 5)


def column_groups():
    groups, start = [], 0
    for k, n in enumerate(SIZES):
        groups.append((start, n, ORDERS[k % 3]))
        start += n
    assert start == FSDP
    return groups


GROUPS = column_groups()
NG = len(GROUPS)


def sylvester(order):
    i = lax.broadcasted_iota(jnp.int32, (order, order), 0)
    j = lax.broadcasted_iota(jnp.int32, (order, order), 1)
    t = jnp.bitwise_and(i, j)
    for s in (4, 2, 1):
        t = jnp.bitwise_xor(t, jnp.right_shift(t, s))
    return (1 - 2 * jnp.bitwise_and(t, 1)).astype(jnp.float32)


def power(exponents):
    return jnp.exp2(exponents.astype(jnp.float32)).astype(jnp.bfloat16)


def kernel(
    local_hbm, outer_hbm, signs_hbm, dexp_hbm, master_hbm, mom_hbm, mexp_hbm,
    out_v, master_o, mom_o,
    lv, ov, sv, so, flips16, dexp_v, thr, master_v, mom_v, mexp_v,
    w1, bd, asrc, abuf, sbuf, srecv,
    *rest,
):
    parts, r1, r2, r3 = (rest[k * NG:(k + 1) * NG] for k in range(4))
    ld_sem, in_sem, rs_send, rs_recv, ag_send, ag_recv, a1_send, a1_recv, a2_sem, reply = rest[4 * NG:]
    c, f = lax.axis_index("cuts"), lax.axis_index("fsdp")
    x, yh = lax.div(c, 2), lax.rem(c, 2)
    v = lax.div(x, 2)
    u = lax.rem(lax.rem(x, 2) + v, 2)
    flip_x = x + 1 - 2 * lax.rem(x, 2)
    partner = (
        (flip_x * 2 + yh, f),
        ((3 - x) * 2 + yh, f),
        (x * 2 + 1 - yh, f),
    )

    def first_row(order, bits):
        mine = [u, v, yh]
        for d, b in zip(order, bits):
            mine[d] = lax.rem(mine[d] + b, 2)
        au, av, ay = mine
        ax = av * 2 + lax.rem(au + av, 2)
        return pl.multiple_of((ax * 2 + ay) * RB, RB)

    half = lax.div(f, FSDP // 2)

    def owner(q):
        return lax.rem(q + half * (FSDP // 2), FSDP)

    def at(q, n):
        return pl.ds(pl.multiple_of(owner(q) * OW, OW), n * OW)

    barrier = pltpu.get_barrier_semaphore()
    for p in partner:
        pl.semaphore_signal(barrier, inc=1, device_id=p, device_id_type=MESH)

    small = [
        pltpu.make_async_copy(signs_hbm.at[:, at(0, FSDP // 2)], sv.at[:, pl.ds(0, DIM // 2)], in_sem.at[0]),
        pltpu.make_async_copy(dexp_hbm.at[0, 0], dexp_v, in_sem.at[1]),
        pltpu.make_async_copy(master_hbm, master_v, in_sem.at[2]),
        pltpu.make_async_copy(mom_hbm, mom_v, in_sem.at[3]),
        pltpu.make_async_copy(mexp_hbm, mexp_v, in_sem.at[4]),
        pltpu.make_async_copy(signs_hbm.at[:, pl.ds(pl.multiple_of(f * OW, OW), OW)], so, in_sem.at[5]),
        pltpu.make_async_copy(signs_hbm.at[:, at(FSDP // 2, FSDP // 2)], sv.at[:, pl.ds(DIM // 2, DIM // 2)], in_sem.at[6]),
    ]
    loads = []
    for g, (start, n, _) in enumerate(GROUPS):
        cols = pl.ds(start * OW, n * OW)
        loads.append((
            pltpu.make_async_copy(local_hbm.at[0, 0, :, at(start, n)], lv.at[:, cols], ld_sem.at[g, 0]),
            pltpu.make_async_copy(outer_hbm.at[0, :, at(start, n)], ov.at[:, cols], ld_sem.at[g, 1]),
        ))
    small[0].start()
    small[1].start()
    small[6].start()
    for pair in loads:
        for cp in pair:
            cp.start()
    for cp in small[2:6]:
        cp.start()

    @pl.loop(f + 1, FSDP)
    def _(to):
        pl.semaphore_signal(barrier, inc=1, device_id=(c, to), device_id_type=MESH)

    table = sylvester(HB)
    table_b = table.astype(jnp.bfloat16)
    w1[0:HB, :] = table_b
    w1[HB:OW, :] = (-table).astype(jnp.bfloat16)
    zero = jnp.zeros((HB, HB), jnp.bfloat16)
    bd[0:HB, 0:HB] = table_b
    bd[HB:OW, HB:OW] = table_b
    bd[0:HB, HB:OW] = zero
    bd[HB:OW, 0:HB] = zero

    small[0].wait()
    small[6].wait()
    for k in range(DIM // OW):
        cols = pl.ds(k * OW, OW)
        row = (1 - 2 * sv[:, cols]).astype(jnp.float32)
        flips16[:, cols] = jnp.broadcast_to(row, (RB, OW)).astype(jnp.bfloat16)
    small[1].wait()
    limits = (power(dexp_v[...]).astype(jnp.float32) * LIMIT).T
    swapped = jnp.concatenate([limits[:, DIM // HB // 2:], limits[:, :DIM // HB // 2]], axis=1)
    thr[...] = jnp.where(half == 0, limits, swapped)

    def deltas(g, part):
        start, n, order = GROUPS[g]
        rows = [first_row(order, (part, j // 2, j % 2)) for j in range(4)]
        tiles = []
        for row in rows:
            for k in range(2 * n):
                cols = pl.ds((2 * start + k) * HB, HB)
                flips = flips16[:, cols]
                o = ov[pl.ds(row, RB), cols] * flips
                l = lv[pl.ds(row, RB), cols] * flips
                tiles.append(jnp.concatenate([o, l], axis=1))
        turned = jnp.dot(jnp.concatenate(tiles, axis=0), w1[...], preferred_element_type=jnp.float32)
        for j, row in enumerate(rows):
            limits = thr[pl.ds(row, RB), :]
            for k in range(2 * n):
                cb = 2 * start + k
                top = jnp.broadcast_to(limits[:, cb:cb + 1], (RB, HB))
                at_row = (j * 2 * n + k) * RB
                value = turned[at_row:at_row + RB, :]
                value = jnp.minimum(jnp.maximum(value, -top), top)
                parts[g][part, j, :, pl.ds(k * HB, HB)] = value.astype(jnp.bfloat16)

    def remote(src, dst, send, recv, to):
        return pltpu.make_async_remote_copy(
            src_ref=src, dst_ref=dst, send_sem=send, recv_sem=recv, device_id=to, device_id_type=MESH
        )

    def rs_copy(g, i):
        to = partner[GROUPS[g][2][(0, 0, 1, 1, 2)[i]]]
        two = (pl.ds(2, 2), pl.ds(0, 2))
        src = (
            lambda: parts[g].at[1, two[0]], lambda: parts[g].at[1, two[1]],
            lambda: parts[g].at[0, 3], lambda: parts[g].at[0, 2], lambda: parts[g].at[0, 1],
        )[i]()
        dst = (
            lambda: r1[g].at[two[0]], lambda: r1[g].at[two[1]],
            lambda: r2[g].at[1], lambda: r2[g].at[0], lambda: r3[g],
        )[i]()
        return remote(src, dst, rs_send.at[g, i], rs_recv.at[g, i], to)

    def ag_copy(g, d, i):
        start, n, order = GROUPS[g]
        row = first_row(order, (0, i // 2, i % 2))
        block = out_v.at[pl.ds(row, RB), at(start, n)]
        slot = (0, 4, 6)[d] + i
        return remote(block, block, ag_send.at[g, slot], ag_recv.at[g, slot], partner[order[d]])

    def add(mine, other):
        return mine.astype(jnp.float32) + other.astype(jnp.float32)

    early, late = range(0, NG // 2), range(NG // 2, NG)
    for g in early:
        for cp in loads[g]:
            cp.wait()
        deltas(g, 1)
        if g == 0:
            pl.semaphore_wait(barrier, 3 + f)
        rs_copy(g, 0).start()
        rs_copy(g, 1).start()
        if g == 0:
            @pl.loop(0, f)
            def _(to):
                other = half - lax.div(to, FSDP // 2)
                pl.semaphore_signal(reply.at[other], inc=1, device_id=(c, to), device_id_type=MESH)

    for cp in small[2:6]:
        cp.wait()
    own = (1 - 2 * so[...]).astype(jnp.float32)

    def prepare(k, carry):
        s = pl.ds(k * 8, 8)
        a = (master_v[s] - KEEP_MOMENTUM * mom_v[s]).reshape(8 * RB, OW) * own
        hi = a.astype(jnp.bfloat16)
        lo = (a - hi.astype(jnp.float32)).astype(jnp.bfloat16)
        turned = jnp.dot(hi, bd[...], preferred_element_type=jnp.float32)
        turned += jnp.dot(lo, bd[...], preferred_element_type=jnp.float32)
        asrc[s, :, 0:OW] = turned.astype(jnp.bfloat16).reshape(8, RB, OW)
        return carry

    lax.fori_loop(0, FSDP // 8, prepare, 0)
    scales = [power(mexp_v[:, b, :]).astype(jnp.float32) for b in range(2)]
    first = lax.broadcasted_iota(jnp.int32, (RB, HB), 1) < HB // 2
    for s in range(FSDP):
        both = jnp.where(
            first,
            jnp.broadcast_to(scales[0][:, s:s + 1], (RB, HB)),
            jnp.broadcast_to(scales[1][:, s:s + 1], (RB, HB)),
        )
        asrc[s, :, OW:OW + HB] = both.astype(jnp.bfloat16)

    def owner_copy(to):
        return remote(asrc.at[to], abuf.at[f], a1_send, a1_recv.at[f], (c, to))

    def owner_send(low, high):
        @pl.loop(low, high)
        def _(to):
            owner_copy(to).start()

    owner_send(0, f)
    abuf[f] = asrc[f]

    for g in early:
        deltas(g, 0)
    for g in late:
        for cp in loads[g]:
            cp.wait()
        deltas(g, 1)

    def acc1(g, low):
        def one(j, carry):
            parts[g][0, j] = add(parts[g][0, j], r1[g][j]).astype(jnp.bfloat16)
            return carry

        lax.fori_loop(low, low + 2, one, 0)

    def stage_a(groups):
        for g in groups:
            rs_copy(g, 0).wait_recv()
            acc1(g, 2)
            rs_copy(g, 2).start()
            rs_copy(g, 3).start()

    def stage_b(groups):
        for g in groups:
            rs_copy(g, 1).wait_recv()
            acc1(g, 0)

    def stage_c(groups):
        for g in groups:
            rs_copy(g, 2).wait_recv()
            parts[g][0, 1] = add(parts[g][0, 1], r2[g][1]).astype(jnp.bfloat16)
            rs_copy(g, 4).start()

    def stage_d(groups):
        for g in groups:
            rs_copy(g, 3).wait_recv()
            parts[g][0, 0] = add(parts[g][0, 0], r2[g][0]).astype(jnp.bfloat16)

    def stage_e(groups):
        for g in groups:
            start, n, order = GROUPS[g]
            rs_copy(g, 4).wait_recv()

            @pl.loop(start, start + n)
            def _(q):
                s = owner(q)

                @pl.when(s != f)
                def _():
                    remote(asrc.at[s], abuf.at[s], a1_send, a1_recv.at[s], (c, s)).wait_recv()

            codes = []
            for k in range(n):
                cols = pl.ds(k * OW, OW)
                s = owner(start + k)
                total = add(parts[g][0, 0, :, cols], r3[g][:, cols])
                sbuf[s] = total.astype(jnp.bfloat16)
                code = abuf[s, :, 0:OW].astype(jnp.float32) - (GRAD_IN_MASTER / CUTS) * total
                scale = abuf[s, :, OW:OW + HB].astype(jnp.float32) * LIMIT
                top = jnp.concatenate(
                    [jnp.broadcast_to(scale[:, b:b + 1], (RB, HB)) for b in (0, HB // 2)], axis=1
                )
                codes.append(jnp.minimum(jnp.maximum(code, -top), top).astype(jnp.bfloat16))
            turned = jnp.dot(jnp.concatenate(codes, axis=0), bd[...], preferred_element_type=jnp.float32)
            row = first_row(order, (0, 0, 0))
            for k in range(n):
                flips = flips16[:, pl.ds((start + k) * OW, OW)].astype(jnp.float32) * (1.0 / HB)
                out_v[pl.ds(row, RB), at(start + k, 1)] = (turned[k * RB:(k + 1) * RB, :] * flips).astype(jnp.bfloat16)
            for d in (2, 1, 0):
                ag_copy(g, d, 0).start()

            @pl.loop(start, start + n)
            def _(q):
                to = owner(q)

                @pl.when(to != f)
                def _():
                    remote(sbuf.at[to], srecv.at[f], a2_sem.at[0], a2_sem.at[1], (c, to)).start()

    def forward1(groups):
        for g in groups:
            ag_copy(g, 2, 0).wait_recv()
            ag_copy(g, 1, 1).start()
            ag_copy(g, 0, 1).start()

    def forward2(groups):
        for g in groups:
            for i in range(2):
                ag_copy(g, 1, i).wait_recv()
                ag_copy(g, 0, 2 + i).start()

    stage_a(early)
    for g in late:
        rs_copy(g, 0).start()
    split = (half + 1) * (FSDP // 2)

    @pl.when(f + 1 < split)
    def _():
        pl.semaphore_wait(reply.at[0], split - 1 - f)
        owner_send(f + 1, split)

    stage_b(early)
    stage_c(early)
    for g in late:
        rs_copy(g, 1).start()
    for g in late:
        deltas(g, 0)
    stage_d(early)
    stage_a(late)
    stage_e(early)

    @pl.when(split < FSDP)
    def _():
        pl.semaphore_wait(reply.at[1], FSDP - split)
        owner_send(split, FSDP)

    stage_b(late)
    stage_c(late)
    stage_d(late)
    forward1(early)
    stage_e(late)
    forward2(early)
    srecv[f] = sbuf[f]
    forward1(late)
    forward2(late)

    others = pl.ds(0, FSDP - 1)
    pltpu.make_async_copy(srecv.at[others], srecv.at[others], a2_sem.at[1]).wait()

    def finish(k, carry):
        s = pl.ds(k * 8, 8)
        turned = jnp.dot(srecv[s].reshape(8 * RB, OW), bd[...], preferred_element_type=jnp.float32)
        grad = (turned * (own * (1.0 / (HB * CUTS)))).reshape(8, RB, OW)
        mom = DECAY * mom_v[s] + grad
        mom_o[s] = mom
        master_o[s] = master_v[s] - OUTER_RATE * (grad + DECAY * mom)
        return carry

    lax.fori_loop(0, FSDP // 8, finish, 0)

    for g in range(NG):
        for i in range(4):
            ag_copy(g, 0, i).wait_recv()
    for g in range(NG):
        for i in range(5):
            rs_copy(g, i).wait_send()
        for d in range(3):
            for i in range((4, 2, 1)[d]):
                ag_copy(g, d, i).wait_send()
    pltpu.make_async_copy(asrc.at[others], asrc.at[others], a1_send).wait()
    pltpu.make_async_copy(sbuf.at[others], sbuf.at[others], a2_sem.at[0]).wait()


def write_out(out_v, master_v, mom_v, out_hbm, master_hbm, mom_hbm, sem):
    copies = [
        pltpu.make_async_copy(out_v.at[pl.ds(k * 32, 32)], out_hbm.at[0, pl.ds(k * 32, 32)], sem.at[k]) for k in range(4)
    ]
    copies += [
        pltpu.make_async_copy(master_v, master_hbm, sem.at[4]),
        pltpu.make_async_copy(mom_v, mom_hbm, sem.at[5]),
    ]
    for cp in copies:
        cp.start()
    for cp in copies:
        cp.wait()


def step(local_params, outer_params, column_signs, delta_exponents, outer_master, outer_momentum, master_exponents):
    bf16, f32, i32 = jnp.bfloat16, jnp.float32, jnp.int32
    widths = [n * OW for _, n, _ in GROUPS]
    anywhere = pl.BlockSpec(memory_space=pl.ANY)
    vmem = pl.BlockSpec(memory_space=pltpu.VMEM)
    state = (FSDP, RB, OW)
    scratch = [
        pltpu.VMEM((ROWS, DIM), bf16),
        pltpu.VMEM((ROWS, DIM), bf16),
        pltpu.VMEM((1, DIM), i32),
        pltpu.VMEM((1, OW), i32),
        pltpu.VMEM((RB, DIM), bf16),
        pltpu.VMEM((DIM // HB, ROWS), i32),
        pltpu.VMEM((ROWS, DIM // HB), f32),
        pltpu.VMEM(state, f32),
        pltpu.VMEM(state, f32),
        pltpu.VMEM((RB, OW // HB, FSDP), i32),
        pltpu.VMEM((OW, HB), bf16),
        pltpu.VMEM((OW, OW), bf16),
        pltpu.VMEM((FSDP, RB, OW + HB), bf16),
        pltpu.VMEM((FSDP, RB, OW + HB), bf16),
        pltpu.VMEM(state, bf16),
        pltpu.VMEM(state, bf16),
    ]
    scratch += [pltpu.VMEM((2, 4, RB, w), bf16) for w in widths]
    scratch += [pltpu.VMEM((4, RB, w), bf16) for w in widths]
    scratch += [pltpu.VMEM((2, RB, w), bf16) for w in widths]
    scratch += [pltpu.VMEM((RB, w), bf16) for w in widths]
    dma = pltpu.SemaphoreType.DMA
    scratch += [
        dma((NG, 2)), dma((7,)), dma((NG, 5)), dma((NG, 5)), dma((NG, 7)), dma((NG, 7)),
        dma, dma((FSDP,)), dma((2,)), pltpu.SemaphoreType.REGULAR((2,)),
    ]
    hbm = functools.partial(pltpu.with_memory_space_constraint, memory_space=pltpu.HBM)
    held = pl.pallas_call(
        kernel,
        out_shape=(pltpu.VMEM((ROWS, DIM), bf16), pltpu.VMEM(state, f32), pltpu.VMEM(state, f32)),
        in_specs=[anywhere] * 7,
        out_specs=(vmem,) * 3,
        scratch_shapes=scratch,
        compiler_params=pltpu.CompilerParams(
            collective_id=0, has_side_effects=True, vmem_limit_bytes=40 * 1024 * 1024
        ),
    )(
        hbm(local_params), hbm(outer_params), hbm(column_signs.reshape(1, DIM)),
        hbm(jnp.swapaxes(delta_exponents, 2, 3)), hbm(outer_master), hbm(outer_momentum),
        hbm(jnp.transpose(master_exponents, (1, 2, 0))),
    )
    return pl.pallas_call(
        write_out,
        out_shape=(
            pltpu.HBM((1, ROWS, DIM), bf16),
            pltpu.HBM(state, f32),
            pltpu.HBM(state, f32),
        ),
        in_specs=[vmem] * 3,
        out_specs=(anywhere,) * 3,
        scratch_shapes=[dma((6,))],
    )(*[pltpu.with_memory_space_constraint(h, pltpu.VMEM) for h in held])


def solution(mesh):
    placed = (
        P("cuts", "fsdp", None, None),
        P("fsdp", None, None),
        P(),
        P("cuts", "fsdp", None, None),
        P(None, "cuts", "fsdp"),
        P(None, "cuts", "fsdp"),
        P(None, "cuts", "fsdp"),
    )
    return jax.shard_map(
        step,
        mesh=mesh,
        in_specs=placed,
        out_specs=(P("fsdp", None, None), P(None, "cuts", "fsdp"), P(None, "cuts", "fsdp")),
        check_vma=False,
    )
```

time: 62.1 us -> 48.9 us (0.79)
  the two profiles are of different devices: /device:TPU:16 before, /device:TPU:224 now
where the time goes in v2:
time: 48.9 us; the launch traced here: 48.8 us
  Pallas kernels  48.2 us (99%)
  between operations  0.64 us (1%)
    pallas_call x1, Pallas kernels, step(): pl.pallas_call(kernel, out_shape=(pltpu.VMEM((ROWS, DIM), bf16), pltpu.VM...  46.5 us
    pallas_call x1, Pallas kernels, step(): pl.pallas_call(write_out, out_shape=(pltpu.HBM((1, ROWS, DIM), bf16), plt...  1.71 us

profile of v2, /device:TPU:224, one launch (start us, length us, event | category | flops | bytes accessed | tf_op | source)
XLA Modules:
  0.0 48.8 jit_solution(11640011201915401838)
XLA Ops:
  0.6 46.5 %shard_map.94 = (bf16[128,8192]{1,0:T(8,128)(2,1)S(1)}, f32[32,16,256]{2,1,0:T(8,128)S(1)}, f32[32,16,256]{2,1,0:T(8,128)S(1)}) custom-call(bf16[1,1,128,8192]{3,2,1,0:T(8,128)(2,1)} %local_hbm.1, bf16[1,128,8192]{2,1,0:T(8,128)(2,1)} %outer_hbm.1, s32[1,8192]{1,0:T(1,128)} %bitcast.3, s32[1,1,64,128]{3,2,1,0:T(8,128)} %bitcast.4, ...), custom_call_target="tpu_custom_call" | custom-call | tf_op jit(solution)/shard_map/pallas_call | solution.py:447
  47.1 1.7 %shard_map.95 = (bf16[1,128,8192]{2,1,0:T(8,128)(2,1)}, f32[32,16,256]{2,1,0:T(8,128)}, f32[32,16,256]{2,1,0:T(8,128)}) custom-call(bf16[128,8192]{1,0:T(8,128)(2,1)S(1)} %get-tuple-element.6.out_v, f32[32,16,256]{2,1,0:T(8,128)S(1)} %get-tuple-element.7.master_v, f32[32,16,256]{2,1,0:T(8,128)S(1)} %get-tuple-element.8.mom_v), custom_call_target="tpu_custom_call" | custom-call | tf_op jit(solution)/shard_map/pallas_call | solution.py:461

commit v3 on v2

v3 whole, which is shorter than its diff:
```python
import functools
import math

import jax
import jax.numpy as jnp
from jax import lax
from jax.experimental import pallas as pl
from jax.experimental.pallas import tpu as pltpu
from jax.sharding import PartitionSpec as P

HB = 128
RB = 16
OW = 256
CUTS = 8
FSDP = 32
DIM = FSDP * OW
ROWS = CUTS * RB
LIMIT = 448.0 * math.sqrt(HB)
OUTER_RATE = 0.7
DECAY = 0.9
KEEP_MOMENTUM = OUTER_RATE * DECAY * DECAY
GRAD_IN_MASTER = OUTER_RATE * (1.0 + DECAY)
MESH = pl.DeviceIdType.MESH

XA, XB, YH = 0, 1, 2
ORDERS = ((XA, XB, YH), (XB, YH, XA), (YH, XA, XB))
SIZES = (6, 6, 4, 6, 4, 6)
PEERS = FSDP // 2


def column_groups():
    groups, start = [], 0
    for k, n in enumerate(SIZES):
        groups.append((start, n, k // 3, ORDERS[k % 3]))
        start += n
    assert start == FSDP
    return groups


GROUPS = column_groups()
NG = len(GROUPS)
EARLY, LATE = range(0, NG // 2), range(NG // 2, NG)


def y_weight(g):
    _, _, cross, order = GROUPS[g]
    return (4, 2, 1)[order.index(YH)] if cross else 0


def bits(i):
    return (i // 4, i // 2 % 2, i % 2)


def sylvester(order):
    i = lax.broadcasted_iota(jnp.int32, (order, order), 0)
    j = lax.broadcasted_iota(jnp.int32, (order, order), 1)
    t = jnp.bitwise_and(i, j)
    for s in (4, 2, 1):
        t = jnp.bitwise_xor(t, jnp.right_shift(t, s))
    return (1 - 2 * jnp.bitwise_and(t, 1)).astype(jnp.float32)


def power(exponents):
    return jnp.exp2(exponents.astype(jnp.float32)).astype(jnp.bfloat16)


def kernel(
    local_hbm, outer_hbm, signs_hbm, dexp_hbm, master_hbm, mom_hbm, mexp_hbm,
    out_v, master_o, mom_o,
    lv, ov, sv, so, flips16, dexp_v, thr, master_v, mom_v, mexp_v,
    w1, bd, asrc, abuf, sbuf, srecv,
    *rest,
):
    parts, r1, r2, r3 = (rest[k * NG:(k + 1) * NG] for k in range(4))
    rest = rest[4 * NG:]
    rx = dict(zip(LATE, rest[:len(LATE)]))
    side = dict(zip(LATE, rest[len(LATE):2 * len(LATE)]))
    ld_sem, in_sem, rs_send, rs_recv, ag_send, ag_recv, a1_send, a1_recv, a2_sem, reply = rest[2 * len(LATE):]
    c, f = lax.axis_index("cuts"), lax.axis_index("fsdp")
    x, yh = lax.div(c, 2), lax.rem(c, 2)
    z, yl, core = lax.div(f, 4), lax.rem(lax.div(f, 2), 2), lax.rem(f, 2)
    v = lax.div(x, 2)
    u = lax.rem(lax.rem(x, 2) + v, 2)
    flip_x = x + 1 - 2 * lax.rem(x, 2)
    sister = z * 4 + (1 - yl) * 2 + core
    partner = (
        (flip_x * 2 + yh, f),
        ((3 - x) * 2 + yh, f),
        (x * 2 + 1 - yh, f),
    )
    near, far = (c, sister), (x * 2 + 1 - yh, sister)
    place = z * 2 + core
    half = lax.div(place, PEERS // 2)

    def peer(m):
        return (c, lax.div(m, 2) * 4 + yl * 2 + lax.rem(m, 2))

    def member(q):
        return lax.rem(q % PEERS // 2 + half * 4, 8) * 2 + q % 2

    def line(q):
        return pl.ds(pl.multiple_of(member(q) * 2 * OW + lax.rem(yl + q // PEERS, 2) * 2 * OW, 2 * OW), 2 * OW)

    def first_row(order, flips):
        mine = [u, v, yh]
        for d, b in zip(order, flips):
            mine[d] = lax.rem(mine[d] + b, 2)
        au, av, ay = mine
        ax = av * 2 + lax.rem(au + av, 2)
        return pl.multiple_of((ax * 2 + ay) * RB, RB)

    barrier = pltpu.get_barrier_semaphore()
    for p in (*partner, near, far):
        pl.semaphore_signal(barrier, inc=1, device_id=p, device_id_type=MESH)

    small = [
        pltpu.make_async_copy(signs_hbm, sv, in_sem.at[0]),
        pltpu.make_async_copy(dexp_hbm.at[0, 0], dexp_v, in_sem.at[1]),
        pltpu.make_async_copy(master_hbm, master_v, in_sem.at[2]),
        pltpu.make_async_copy(mom_hbm, mom_v, in_sem.at[3]),
        pltpu.make_async_copy(mexp_hbm, mexp_v, in_sem.at[4]),
        pltpu.make_async_copy(signs_hbm.at[:, pl.ds(pl.multiple_of(f * OW, OW), OW)], so, in_sem.at[5]),
    ]
    loads = []
    for q in range(0, FSDP, 2):
        cols, source = pl.ds(q * OW, 2 * OW), line(q)
        loads.append((
            pltpu.make_async_copy(local_hbm.at[0, 0, :, source], lv.at[:, cols], ld_sem.at[q // 2, 0]),
            pltpu.make_async_copy(outer_hbm.at[0, :, source], ov.at[:, cols], ld_sem.at[q // 2, 1]),
        ))
    small[0].start()
    small[1].start()
    for pair in loads[:PEERS // 2]:
        for cp in pair:
            cp.start()
    for cp in small[2:]:
        cp.start()
    for pair in loads[PEERS // 2:]:
        for cp in pair:
            cp.start()

    @pl.loop(place + 1, PEERS)
    def _(m):
        pl.semaphore_signal(barrier, inc=1, device_id=peer(m), device_id_type=MESH)

    table = sylvester(HB)
    table_b = table.astype(jnp.bfloat16)
    w1[0:HB, :] = table_b
    w1[HB:OW, :] = (-table).astype(jnp.bfloat16)
    zero = jnp.zeros((HB, HB), jnp.bfloat16)
    bd[0:HB, 0:HB] = table_b
    bd[HB:OW, HB:OW] = table_b
    bd[0:HB, HB:OW] = zero
    bd[HB:OW, 0:HB] = zero

    small[0].wait()
    for q in range(0, FSDP, 2):
        row = (1 - 2 * sv[:, line(q)]).astype(jnp.float32)
        flips16[:, pl.ds(q * OW, 2 * OW)] = jnp.broadcast_to(row, (RB, 2 * OW)).astype(jnp.bfloat16)
    blocks = DIM // HB
    block = lax.broadcasted_iota(jnp.int32, (blocks, blocks), 0)
    spot = lax.broadcasted_iota(jnp.int32, (blocks, blocks), 1)
    cross = jnp.bitwise_and(jnp.right_shift(spot, 5) + yl, 1)
    wanted = jnp.bitwise_and(jnp.right_shift(spot, 2) + half * 4, 7) * 8 + cross * 4 + jnp.bitwise_and(spot, 3)
    move = jnp.where(block == wanted, 1.0, 0.0).astype(jnp.bfloat16)
    small[1].wait()
    powers = power(dexp_v[...]).astype(jnp.float32).T.astype(jnp.bfloat16)
    thr[...] = jnp.dot(powers, move, preferred_element_type=jnp.float32) * LIMIT

    def deltas(g, part):
        start, n, _, order = GROUPS[g]
        rows = [first_row(order, (part, j // 2, j % 2)) for j in range(4)]
        tiles = []
        for row in rows:
            for k in range(2 * n):
                cols = pl.ds((2 * start + k) * HB, HB)
                flips = flips16[:, cols]
                o = ov[pl.ds(row, RB), cols] * flips
                l = lv[pl.ds(row, RB), cols] * flips
                tiles.append(jnp.concatenate([o, l], axis=1))
        turned = jnp.dot(jnp.concatenate(tiles, axis=0), w1[...], preferred_element_type=jnp.float32)
        for j, row in enumerate(rows):
            limits = thr[pl.ds(row, RB), :]
            for k in range(2 * n):
                cb = 2 * start + k
                top = jnp.broadcast_to(limits[:, cb:cb + 1], (RB, HB))
                at_row = (j * 2 * n + k) * RB
                value = turned[at_row:at_row + RB, :]
                value = jnp.minimum(jnp.maximum(value, -top), top)
                parts[g][part, j, :, pl.ds(k * HB, HB)] = value.astype(jnp.bfloat16)

    def load(g):
        start, n, _, _ = GROUPS[g]
        for pair in loads[start // 2:(start + n) // 2]:
            for cp in pair:
                cp.wait()

    def remote(src, dst, send, recv, to):
        return pltpu.make_async_remote_copy(
            src_ref=src, dst_ref=dst, send_sem=send, recv_sem=recv, device_id=to, device_id_type=MESH
        )

    def kept1(g, j):
        return rx[g].at[j] if y_weight(g) == 4 else parts[g].at[0, j]

    def kept2(g, j):
        return rx[g].at[j] if y_weight(g) == 2 else kept1(g, j)

    def kept3(g):
        return rx[g].at[0] if y_weight(g) == 1 else kept2(g, 0)

    def rs_copies(g, i):
        level = (0, 0, 1, 1, 2)[i]
        order = GROUPS[g][3]
        two = pl.ds((2, 0)[i], 2) if i < 2 else None
        one = (None, None, 1, 0, None)[i]
        dst = (lambda: r1[g].at[two], lambda: r2[g].at[one], lambda: r3[g])[level]()
        sources = [
            (lambda: parts[g].at[b, two], lambda: kept1(g, 2 * b + one), lambda: kept2(g, b))[level]() for b in range(2)
        ]
        if y_weight(g) != (4, 2, 1)[level]:
            return [remote(sources[1], dst, rs_send.at[g, i], rs_recv.at[g, i], partner[order[level]])]
        other = (lambda: rx[g].at[two], lambda: rx[g].at[one], lambda: rx[g].at[0])[level]()
        return [
            remote(sources[1], dst, rs_send.at[g, i], rs_recv.at[g, i], far),
            remote(sources[0], other, rs_send.at[g, 5 + i], rs_recv.at[g, 5 + i], near),
        ]

    def rs_start(g, i):
        for cp in rs_copies(g, i):
            cp.start()

    def rs_wait(g, i):
        for cp in rs_copies(g, i):
            cp.wait_recv()

    def block_of(g, i):
        start, n, _, order = GROUPS[g]
        return out_v.at[pl.ds(first_row(order, bits(i)), RB), pl.ds(start * OW, n * OW)]

    def ag_slots(g, slot):
        return ag_send.at[g, slot], ag_recv.at[g, slot]

    def ag_from_side(g, i):
        yb, order = y_weight(g), GROUPS[g][3]
        found = []
        for w in (1, 2, 4):
            if i < w < yb:
                to = partner[order[{4: 0, 2: 1, 1: 2}[w]]]
                found.append(remote(side[g].at[i], side[g].at[i + w], *ag_slots(g, 8 + i + w), to))
        found.append(remote(side[g].at[i], block_of(g, i), *ag_slots(g, i), near))
        found.append(remote(side[g].at[i], block_of(g, i), *ag_slots(g, i + yb), far))
        return found

    def ag_from_block(g, i):
        yb, order = y_weight(g), GROUPS[g][3]
        found = []
        for w in (1, 2, 4):
            if w > i and w >= 2 * yb:
                to = partner[order[{4: 0, 2: 1, 1: 2}[w]]]
                found.append(remote(block_of(g, i), block_of(g, i), *ag_slots(g, i + w), to))
        return found

    def ag_arrive(g, slot):
        ref = side[g].at[slot - 8] if slot >= 8 else block_of(g, slot)
        remote(ref, ref, *ag_slots(g, slot), near).wait_recv()

    def ag_pass_on(g, slot):
        ag_arrive(g, slot)
        for cp in ag_from_side(g, slot - 8) if slot >= 8 else ag_from_block(g, slot):
            cp.start()

    def add(mine, other):
        return mine.astype(jnp.float32) + other.astype(jnp.float32)

    pl.semaphore_wait(barrier, 5 + place)

    @pl.loop(0, place)
    def _(m):
        other = half - lax.div(m, PEERS // 2)
        pl.semaphore_signal(reply.at[other], inc=1, device_id=peer(m), device_id_type=MESH)

    for g in EARLY:
        load(g)
        deltas(g, 1)
        rs_start(g, 0)
        rs_start(g, 1)

    for cp in small[2:]:
        cp.wait()
    own = (1 - 2 * so[...]).astype(jnp.float32)

    def prepare(k, carry):
        s = pl.ds(k * 8, 8)
        a = (master_v[s] - KEEP_MOMENTUM * mom_v[s]).reshape(8 * RB, OW) * own
        hi = a.astype(jnp.bfloat16)
        lo = (a - hi.astype(jnp.float32)).astype(jnp.bfloat16)
        turned = jnp.dot(hi, bd[...], preferred_element_type=jnp.float32)
        turned += jnp.dot(lo, bd[...], preferred_element_type=jnp.float32)
        turned = turned.astype(jnp.bfloat16)
        for t in range(8):
            to, which = k * 4 + t // 4 * 2 + t % 2, lax.rem(t // 2 % 2 + yl, 2)
            asrc[to, which, :, 0:OW] = turned[t * RB:(t + 1) * RB, :]
        return carry

    lax.fori_loop(0, FSDP // 8, prepare, 0)
    scales = [power(mexp_v[:, b, :]).astype(jnp.float32) for b in range(2)]
    first = lax.broadcasted_iota(jnp.int32, (RB, HB), 1) < HB // 2
    for s in range(FSDP):
        both = jnp.where(
            first,
            jnp.broadcast_to(scales[0][:, s:s + 1], (RB, HB)),
            jnp.broadcast_to(scales[1][:, s:s + 1], (RB, HB)),
        )
        to, which = s // 4 * 2 + s % 2, lax.rem(s // 2 % 2 + yl, 2)
        asrc[to, which, :, OW:OW + HB] = both.astype(jnp.bfloat16)

    def owner_send(low, high):
        @pl.loop(low, high)
        def _(m):
            remote(asrc.at[m], abuf.at[place], a1_send, a1_recv.at[place], peer(m)).start()

    owner_send(0, place)
    abuf[place] = asrc[place]

    for g in EARLY:
        deltas(g, 0)

    def stage_a(groups):
        for g in groups:
            rs_wait(g, 0)
            for j in (3, 2):
                kept1(g, j)[...] = add(kept1(g, j)[...], r1[g][j]).astype(jnp.bfloat16)
            if y_weight(g) != 2:
                rs_start(g, 2)
                rs_start(g, 3)

    def stage_b(groups):
        for g in groups:
            rs_wait(g, 1)
            for j in (1, 0):
                kept1(g, j)[...] = add(kept1(g, j)[...], r1[g][j]).astype(jnp.bfloat16)
            if y_weight(g) == 2:
                rs_start(g, 2)
                rs_start(g, 3)

    def stage_c(groups):
        for g in groups:
            rs_wait(g, 2)
            kept2(g, 1)[...] = add(kept2(g, 1)[...], r2[g][1]).astype(jnp.bfloat16)
            if y_weight(g) != 1:
                rs_start(g, 4)

    def stage_d(groups):
        for g in groups:
            rs_wait(g, 3)
            kept2(g, 0)[...] = add(kept2(g, 0)[...], r2[g][0]).astype(jnp.bfloat16)
            if y_weight(g) == 1:
                rs_start(g, 4)

    def stage_e(groups):
        for g in groups:
            start, n, cross, order = GROUPS[g]
            low = start % PEERS
            rs_wait(g, 4)
            if not cross:
                for k in range(n):
                    m = member(low + k)

                    @pl.when(m != place)
                    def _():
                        remote(asrc.at[m], abuf.at[m], a1_send, a1_recv.at[m], peer(m)).wait_recv()

            codes = []
            for k in range(n):
                cols = pl.ds(k * OW, OW)
                total = add(kept3(g)[:, cols], r3[g][:, cols])
                m = member(low + k)
                sbuf[m, cross] = total.astype(jnp.bfloat16)
                code = abuf[m, cross, :, 0:OW].astype(jnp.float32) - (GRAD_IN_MASTER / CUTS) * total
                scale = abuf[m, cross, :, OW:OW + HB].astype(jnp.float32) * LIMIT
                top = jnp.concatenate(
                    [jnp.broadcast_to(scale[:, b:b + 1], (RB, HB)) for b in (0, HB // 2)], axis=1
                )
                codes.append(jnp.minimum(jnp.maximum(code, -top), top).astype(jnp.bfloat16))
            turned = jnp.dot(jnp.concatenate(codes, axis=0), bd[...], preferred_element_type=jnp.float32)
            row = first_row(order, (0, 0, 0))
            for k in range(n):
                flips = flips16[:, pl.ds((low + k) * OW, OW)].astype(jnp.float32) * (1.0 / HB)
                value = (turned[k * RB:(k + 1) * RB, :] * flips).astype(jnp.bfloat16)
                if cross:
                    side[g][0, :, pl.ds(k * OW, OW)] = value
                else:
                    out_v[pl.ds(row, RB), pl.ds((start + k) * OW, OW)] = value
            for cp in ag_from_side(g, 0) if cross else ag_from_block(g, 0):
                cp.start()

            for k in range(n):
                m = member(low + k)

                @pl.when(m != place)
                def _():
                    remote(
                        sbuf.at[m, cross], srecv.at[place, cross], a2_sem.at[0], a2_sem.at[1], peer(m)
                    ).start()

    def arrivals(g):
        return {
            0: ((1,), (2, 3), (4, 5, 6, 7)),
            1: ((0, 1), (2, 3), (4, 5, 6, 7)),
            2: ((9,), (0, 2, 1, 3), (4, 5, 6, 7)),
            4: ((9,), (10, 11), (0, 4, 1, 5, 2, 6, 3, 7)),
        }[y_weight(g)]

    def forward(level, groups):
        for g in groups:
            for slot in arrivals(g)[level]:
                ag_pass_on(g, slot)

    split = (half + 1) * (PEERS // 2)

    @pl.when(place + 1 < split)
    def _():
        pl.semaphore_wait(reply.at[0], split - 1 - place)
        owner_send(place + 1, split)

    stage_a(EARLY)
    for g in LATE:
        load(g)
        deltas(g, 1)
        if y_weight(g) == 4:
            deltas(g, 0)
        rs_start(g, 0)
        rs_start(g, 1)
    stage_b(EARLY)
    stage_c(EARLY)
    for g in LATE:
        if y_weight(g) != 4:
            deltas(g, 0)

    @pl.when(split < PEERS)
    def _():
        pl.semaphore_wait(reply.at[1], PEERS - split)
        owner_send(split, PEERS)

    stage_d(EARLY)
    stage_a(LATE)
    stage_b(LATE)
    stage_e(EARLY[:1])
    stage_c(LATE)
    stage_d(LATE)
    stage_e(EARLY[1:])
    forward(0, EARLY)
    stage_e(LATE)
    forward(1, EARLY)
    srecv[place] = sbuf[place]
    forward(0, LATE)
    forward(1, LATE)

    others = pl.ds(0, PEERS - 1)
    pltpu.make_async_copy(srecv.at[others], srecv.at[others], a2_sem.at[1]).wait()

    def finish(k, carry):
        s = pl.ds(k * 8, 8)
        sums = [srecv[k * 4 + t // 4 * 2 + t % 2, lax.rem(t // 2 % 2 + yl, 2)] for t in range(8)]
        turned = jnp.dot(jnp.concatenate(sums, axis=0), bd[...], preferred_element_type=jnp.float32)
        grad = (turned * (own * (1.0 / (HB * CUTS)))).reshape(8, RB, OW)
        mom = DECAY * mom_v[s] + grad
        mom_o[s] = mom
        master_o[s] = master_v[s] - OUTER_RATE * (grad + DECAY * mom)
        return carry

    lax.fori_loop(0, FSDP // 8, finish, 0)

    for g in range(NG):
        for slot in arrivals(g)[2]:
            ag_arrive(g, slot)
    for g in range(NG):
        for i in range(5):
            for cp in rs_copies(g, i):
                cp.wait_send()
        for i in range(y_weight(g)):
            for cp in ag_from_side(g, i):
                cp.wait_send()
        for i in range(4):
            for cp in ag_from_block(g, i):
                cp.wait_send()
    pltpu.make_async_copy(asrc.at[others], asrc.at[others], a1_send).wait()
    pltpu.make_async_copy(sbuf.at[others], sbuf.at[others], a2_sem.at[0]).wait()


def write_out(out_v, master_v, mom_v, out_hbm, master_hbm, mom_hbm, sem):
    f = lax.axis_index("fsdp")
    yl, half = lax.rem(lax.div(f, 2), 2), lax.div(f, FSDP // 2)
    copies = []
    for q in range(0, FSDP, 2):
        oz = lax.rem(q % PEERS // 2 + half * 4, 8)
        cols = pl.multiple_of(oz * 4 * OW + lax.rem(yl + q // PEERS, 2) * 2 * OW, 2 * OW)
        copies.append(pltpu.make_async_copy(
            out_v.at[:, pl.ds(q * OW, 2 * OW)], out_hbm.at[0, :, pl.ds(cols, 2 * OW)], sem.at[q // 2]
        ))
    copies += [
        pltpu.make_async_copy(master_v, master_hbm, sem.at[PEERS]),
        pltpu.make_async_copy(mom_v, mom_hbm, sem.at[PEERS + 1]),
    ]
    for cp in copies:
        cp.start()
    for cp in copies:
        cp.wait()


def step(local_params, outer_params, column_signs, delta_exponents, outer_master, outer_momentum, master_exponents):
    bf16, f32, i32 = jnp.bfloat16, jnp.float32, jnp.int32
    widths = [n * OW for _, n, _, _ in GROUPS]
    anywhere = pl.BlockSpec(memory_space=pl.ANY)
    vmem = pl.BlockSpec(memory_space=pltpu.VMEM)
    state = (FSDP, RB, OW)
    scratch = [
        pltpu.VMEM((ROWS, DIM), bf16),
        pltpu.VMEM((ROWS, DIM), bf16),
        pltpu.VMEM((1, DIM), i32),
        pltpu.VMEM((1, OW), i32),
        pltpu.VMEM((RB, DIM), bf16),
        pltpu.VMEM((DIM // HB, ROWS), i32),
        pltpu.VMEM((ROWS, DIM // HB), f32),
        pltpu.VMEM(state, f32),
        pltpu.VMEM(state, f32),
        pltpu.VMEM((RB, OW // HB, FSDP), i32),
        pltpu.VMEM((OW, HB), bf16),
        pltpu.VMEM((OW, OW), bf16),
        pltpu.VMEM((PEERS, 2, RB, OW + HB), bf16),
        pltpu.VMEM((PEERS, 2, RB, OW + HB), bf16),
        pltpu.VMEM((PEERS, 2, RB, OW), bf16),
        pltpu.VMEM((PEERS, 2, RB, OW), bf16),
    ]
    scratch += [pltpu.VMEM((2, 4, RB, w), bf16) for w in widths]
    scratch += [pltpu.VMEM((4, RB, w), bf16) for w in widths]
    scratch += [pltpu.VMEM((2, RB, w), bf16) for w in widths]
    scratch += [pltpu.VMEM((RB, w), bf16) for w in widths]
    scratch += [pltpu.VMEM((y_weight(g), RB, widths[g]), bf16) for g in LATE] * 2
    dma = pltpu.SemaphoreType.DMA
    scratch += [
        dma((PEERS, 2)), dma((6,)), dma((NG, 10)), dma((NG, 10)), dma((NG, 12)), dma((NG, 12)),
        dma, dma((PEERS,)), dma((2,)), pltpu.SemaphoreType.REGULAR((2,)),
    ]
    hbm = functools.partial(pltpu.with_memory_space_constraint, memory_space=pltpu.HBM)
    held = pl.pallas_call(
        kernel,
        out_shape=(pltpu.VMEM((ROWS, DIM), bf16), pltpu.VMEM(state, f32), pltpu.VMEM(state, f32)),
        in_specs=[anywhere] * 7,
        out_specs=(vmem,) * 3,
        scratch_shapes=scratch,
        compiler_params=pltpu.CompilerParams(
            collective_id=0, has_side_effects=True, vmem_limit_bytes=40 * 1024 * 1024
        ),
    )(
        hbm(local_params), hbm(outer_params), hbm(column_signs.reshape(1, DIM)),
        hbm(jnp.swapaxes(delta_exponents, 2, 3)), hbm(outer_master), hbm(outer_momentum),
        hbm(jnp.transpose(master_exponents, (1, 2, 0))),
    )
    return pl.pallas_call(
        write_out,
        out_shape=(
            pltpu.HBM((1, ROWS, DIM), bf16),
            pltpu.HBM(state, f32),
            pltpu.HBM(state, f32),
        ),
        in_specs=[vmem] * 3,
        out_specs=(anywhere,) * 3,
        scratch_shapes=[dma((PEERS + 2,))],
    )(*[pltpu.with_memory_space_constraint(h, pltpu.VMEM) for h in held])


def solution(mesh):
    placed = (
        P("cuts", "fsdp", None, None),
        P("fsdp", None, None),
        P(),
        P("cuts", "fsdp", None, None),
        P(None, "cuts", "fsdp"),
        P(None, "cuts", "fsdp"),
        P(None, "cuts", "fsdp"),
    )
    return jax.shard_map(
        step,
        mesh=mesh,
        in_specs=placed,
        out_specs=(P("fsdp", None, None), P(None, "cuts", "fsdp"), P(None, "cuts", "fsdp")),
        check_vma=False,
    )
```

time: 48.9 us -> 47.1 us (0.963)
  the two profiles are of different devices: /device:TPU:224 before, /device:TPU:200 now
where the time goes in v3:
time: 47.1 us
  Pallas kernels  46.4 us (99%)
  between operations  0.64 us (1%)
    pallas_call x1, Pallas kernels, step(): pl.pallas_call(kernel, out_shape=(pltpu.VMEM((ROWS, DIM), bf16), pltpu.VM...  44.6 us
    pallas_call x1, Pallas kernels, step(): pl.pallas_call(write_out, out_shape=(pltpu.HBM((1, ROWS, DIM), bf16), plt...  1.83 us

profile of v3, /device:TPU:200, one launch (start us, length us, event | category | flops | bytes accessed | tf_op | source)
XLA Modules:
  0.0 47.1 jit_solution(16880273411252319608)
XLA Ops:
  0.6 44.6 %shard_map.94 = (bf16[128,8192]{1,0:T(8,128)(2,1)S(1)}, f32[32,16,256]{2,1,0:T(8,128)S(1)}, f32[32,16,256]{2,1,0:T(8,128)S(1)}) custom-call(bf16[1,1,128,8192]{3,2,1,0:T(8,128)(2,1)} %local_hbm.1, bf16[1,128,8192]{2,1,0:T(8,128)(2,1)} %outer_hbm.1, s32[1,8192]{1,0:T(1,128)} %bitcast.3, s32[1,1,64,128]{3,2,1,0:T(8,128)} %bitcast.4, ...), custom_call_target="tpu_custom_call" | custom-call | tf_op jit(solution)/shard_map/pallas_call | solution.py:547
  45.2 1.8 %shard_map.95 = (bf16[1,128,8192]{2,1,0:T(8,128)(2,1)}, f32[32,16,256]{2,1,0:T(8,128)}, f32[32,16,256]{2,1,0:T(8,128)}) custom-call(bf16[128,8192]{1,0:T(8,128)(2,1)S(1)} %get-tuple-element.6.out_v, f32[32,16,256]{2,1,0:T(8,128)S(1)} %get-tuple-element.7.master_v, f32[32,16,256]{2,1,0:T(8,128)S(1)} %get-tuple-element.8.mom_v), custom_call_target="tpu_custom_call" | custom-call | tf_op jit(solution)/shard_map/pallas_call | solution.py:561

commit v4 on v3

--- a/solution.py
+++ b/solution.py
@@ -438,17 +438,20 @@
         if y_weight(g) != 4:
             deltas(g, 0)
 
+    stage_d(EARLY)
+
     @pl.when(split < PEERS)
     def _():
         pl.semaphore_wait(reply.at[1], PEERS - split)
         owner_send(split, PEERS)
 
-    stage_d(EARLY)
-    stage_a(LATE)
-    stage_b(LATE)
+    for g in LATE:
+        stage_a([g])
+        stage_b([g])
     stage_e(EARLY[:1])
-    stage_c(LATE)
-    stage_d(LATE)
+    for g in LATE:
+        stage_c([g])
+        stage_d([g])
     stage_e(EARLY[1:])
     forward(0, EARLY)
     stage_e(LATE)

time: 47.1 us -> 46.6 us (0.989); the launches traced: 47.1 us -> 46 us
  Pallas kernels: 46.4 us -> 45.3 us
    pallas_call x1, Pallas kernels: 44.6 us -> 43.5 us  [step(): pl.pallas_call(kernel, out_shape=(pltpu.VMEM((ROWS, DIM), bf16), pltpu.VM...]
where the time goes in v4:
time: 46.6 us; the launch traced here: 46 us
  Pallas kernels  45.3 us (97%)
  between operations  0.64 us (1%)
    pallas_call x1, Pallas kernels, step(): pl.pallas_call(kernel, out_shape=(pltpu.VMEM((ROWS, DIM), bf16), pltpu.VM...  43.5 us
    pallas_call x1, Pallas kernels, step(): pl.pallas_call(write_out, out_shape=(pltpu.HBM((1, ROWS, DIM), bf16), plt...  1.83 us

profile of v4, /device:TPU:200, one launch (start us, length us, event | category | flops | bytes accessed | tf_op | source)
XLA Modules:
  0.0 46.0 jit_solution(6043192773183162380)
XLA Ops:
  0.6 43.5 %shard_map.94 = (bf16[128,8192]{1,0:T(8,128)(2,1)S(1)}, f32[32,16,256]{2,1,0:T(8,128)S(1)}, f32[32,16,256]{2,1,0:T(8,128)S(1)}) custom-call(bf16[1,1,128,8192]{3,2,1,0:T(8,128)(2,1)} %local_hbm.1, bf16[1,128,8192]{2,1,0:T(8,128)(2,1)} %outer_hbm.1, s32[1,8192]{1,0:T(1,128)} %bitcast.3, s32[1,1,64,128]{3,2,1,0:T(8,128)} %bitcast.4, ...), custom_call_target="tpu_custom_call" | custom-call | tf_op jit(solution)/shard_map/pallas_call | solution.py:550
  44.2 1.8 %shard_map.95 = (bf16[1,128,8192]{2,1,0:T(8,128)(2,1)}, f32[32,16,256]{2,1,0:T(8,128)}, f32[32,16,256]{2,1,0:T(8,128)}) custom-call(bf16[128,8192]{1,0:T(8,128)(2,1)S(1)} %get-tuple-element.6.out_v, f32[32,16,256]{2,1,0:T(8,128)S(1)} %get-tuple-element.7.master_v, f32[32,16,256]{2,1,0:T(8,128)S(1)} %get-tuple-element.8.mom_v), custom_call_target="tpu_custom_call" | custom-call | tf_op jit(solution)/shard_map/pallas_call | solution.py:564

commit v5 on v4

--- a/solution.py
+++ b/solution.py
@@ -273,16 +273,17 @@
     def add(mine, other):
         return mine.astype(jnp.float32) + other.astype(jnp.float32)
 
-    pl.semaphore_wait(barrier, 5 + place)
-
-    @pl.loop(0, place)
-    def _(m):
-        other = half - lax.div(m, PEERS // 2)
-        pl.semaphore_signal(reply.at[other], inc=1, device_id=peer(m), device_id_type=MESH)
-
     for g in EARLY:
         load(g)
         deltas(g, 1)
+        if g == 0:
+            pl.semaphore_wait(barrier, 5 + place)
+
+            @pl.loop(0, place)
+            def _(m):
+                other = half - lax.div(m, PEERS // 2)
+                pl.semaphore_signal(reply.at[other], inc=1, device_id=peer(m), device_id_type=MESH)
+
         rs_start(g, 0)
         rs_start(g, 1)
 

time: 46.6 us -> 46.7 us (level)
  the two profiles are of different devices: /device:TPU:200 before, /device:TPU:160 now
where the time goes in v5:
time: 46.7 us; the launch traced here: 46.6 us
  Pallas kernels  46 us (99%)
  between operations  0.64 us (1%)
    pallas_call x1, Pallas kernels, step(): pl.pallas_call(kernel, out_shape=(pltpu.VMEM((ROWS, DIM), bf16), pltpu.VM...  44.1 us
    pallas_call x1, Pallas kernels, step(): pl.pallas_call(write_out, out_shape=(pltpu.HBM((1, ROWS, DIM), bf16), plt...  1.83 us

profile of v5, /device:TPU:160, one launch (start us, length us, event | category | flops | bytes accessed | tf_op | source)
XLA Modules:
  0.0 46.6 jit_solution(3740165438553743207)
XLA Ops:
  0.6 44.1 %shard_map.94 = (bf16[128,8192]{1,0:T(8,128)(2,1)S(1)}, f32[32,16,256]{2,1,0:T(8,128)S(1)}, f32[32,16,256]{2,1,0:T(8,128)S(1)}) custom-call(bf16[1,1,128,8192]{3,2,1,0:T(8,128)(2,1)} %local_hbm.1, bf16[1,128,8192]{2,1,0:T(8,128)(2,1)} %outer_hbm.1, s32[1,8192]{1,0:T(1,128)} %bitcast.3, s32[1,1,64,128]{3,2,1,0:T(8,128)} %bitcast.4, ...), custom_call_target="tpu_custom_call" | custom-call | tf_op jit(solution)/shard_map/pallas_call | solution.py:551
  44.8 1.8 %shard_map.95 = (bf16[1,128,8192]{2,1,0:T(8,128)(2,1)}, f32[32,16,256]{2,1,0:T(8,128)}, f32[32,16,256]{2,1,0:T(8,128)}) custom-call(bf16[128,8192]{1,0:T(8,128)(2,1)S(1)} %get-tuple-element.6.out_v, f32[32,16,256]{2,1,0:T(8,128)S(1)} %get-tuple-element.7.master_v, f32[32,16,256]{2,1,0:T(8,128)S(1)} %get-tuple-element.8.mom_v), custom_call_target="tpu_custom_call" | custom-call | tf_op jit(solution)/shard_map/pallas_call | solution.py:565
